TPU v7x, 32 devices: a whole 2x2x4 slice. The times are simulated.
32 devices in a mesh: groups: 2 (over x), outer: 4 (over z), inner: 4 (over y, core).
Axes of the slice: x: 2, y: 2, z: 4, core: 2. Of those that a mesh axis runs over, the one named last changes fastest.
Arguments:
- q_proj: bfloat16 [16384, 2048], P(('groups', 'outer', 'inner')), parts along dimension 0, may hold values from -4 to 4
- k_proj: bfloat16 [16384, 512], P(('groups', 'outer', 'inner')), parts along dimension 0, may hold values from -4 to 4
- v_proj: bfloat16 [16384, 512], P(('groups', 'outer', 'inner')), parts along dimension 0, may hold values from -6 to 6
- q_taps: float32 [3, 2048], replicated, may hold values from 0.5 to 1.5
- k_taps: float32 [3, 512], replicated, may hold values from 0.5 to 1.5
- v_taps: float32 [3, 512], replicated, may hold values from 0.5 to 1.5
- block_list: int32 [128, 3], P(('groups', 'outer', 'inner')), parts along dimension 0, may hold values from -1 to 63, as said below
Outputs:
- attn_out: bfloat16 [16384, 2048], P(('groups', 'outer', 'inner')), parts along dimension 0
There are 2 independent parts, one for each index of `groups`. A program takes and returns all parts, laid end to end along the dimension named above; an argument that names none is the same for every part. Nothing has to cross between parts.
Inputs may be any that keep to these rules, and one draw needn't show every extreme that they name: `block_list`: row a holds block a and the 1 block before it that exist, then every block b <= a - 2 with b % 64 equal to a phase shared by all rows of a part, the phase below 62; all other entries are -1, and the last row has none.
All inputs are finite; a program needn't handle non-finite values.
Results may differ from a plain program's by a relative error of at most 0.002.
The roundings to bfloat16 on the way count: a program that leaves them out, or rounds other values in their place, can miss the bound.
Values may be sent and summed in bfloat16 or wider, within the bound.
A program may use at most 64 MiB of HBM per device.

v0:
```python
import functools
import math

import jax
import jax.numpy as jnp
from jax import lax
from jax.experimental import pallas as pl
from jax.experimental.pallas import tpu as pltpu
from jax.sharding import PartitionSpec as P

HEAD_DIM = 128
BLOCK = 128
LOCAL = 2
STRIDE = 64
HALO = 16
NEG = -1e30
MESH = pl.DeviceIdType.MESH
SCALE = math.log2(math.e) / math.sqrt(HEAD_DIM)
NT = (((1,), (1,)), ((), ()))


def conv(padded, taps):
    wide = padded.astype(jnp.float32)
    total = taps[0:1] * wide[HALO:]
    for j in (1, 2):
        total = total + taps[j : j + 1] * pltpu.roll(wide, j, 0)[HALO:]
    return total.astype(jnp.bfloat16)


def kernel(
    ni, no, list_hbm, q_hbm, k_hbm, v_hbm, qt_hbm, kt_hbm, vt_hbm, outb,
    list_ref, qt_ref, kt_ref, vt_ref, qpad, kvpad, kvc, qs, acc_ref, max_ref, pbuf, wout, win, cand, rbuf, zpiece, zbuf,
    fsum, far, in_sem, tail_s, tail_r, w_s, w_r, sc_s, sc_r, z_s, z_r,
    g_s, g_r,
):
    tokens, qw = q_hbm.shape
    kvw = k_hbm.shape[1]
    groups = kvw // HEAD_DIM
    per_group = qw // kvw
    nb = tokens // BLOCK
    slots = far.shape[1]
    piece_rows, piece_cols = zpiece.shape[1:]
    col_parts = kvw // piece_cols
    before = BLOCK + HALO
    entries = list_ref.shape[1]
    o = lax.axis_index("outer")
    i = lax.axis_index("inner")
    d = o * ni + i
    last = ni * no - 1
    has_next = d < last
    has_prev = d > 0

    def chain(step):
        other = d + step
        return {"outer": other // ni, "inner": lax.rem(other, ni)}

    def inner_peer(r):
        return {"inner": lax.rem(i + r, ni)}

    loads = [
        pltpu.make_async_copy(q_hbm, qpad.at[pl.ds(HALO, tokens)], in_sem.at[0]),
        pltpu.make_async_copy(k_hbm, kvpad.at[0, pl.ds(before, tokens)], in_sem.at[1]),
        pltpu.make_async_copy(v_hbm, kvpad.at[1, pl.ds(before, tokens)], in_sem.at[2]),
        pltpu.make_async_copy(list_hbm, list_ref, in_sem.at[3]),
        pltpu.make_async_copy(qt_hbm, qt_ref, in_sem.at[4]),
        pltpu.make_async_copy(kt_hbm, kt_ref, in_sem.at[5]),
        pltpu.make_async_copy(vt_hbm, vt_ref, in_sem.at[6]),
    ]
    for n in (3, 1, 5, 2, 6, 0, 4):
        loads[n].start()

    barrier = pltpu.get_barrier_semaphore()
    for r in range(1, ni):
        pl.semaphore_signal(barrier, inc=1, device_id=inner_peer(r), device_id_type=MESH)
    for r in range(1, no):
        pl.semaphore_signal(
            barrier, inc=1, device_id={"outer": lax.rem(o + r, no)}, device_id_type=MESH
        )

    @pl.when(has_next)
    def _():
        pl.semaphore_signal(barrier, inc=1, device_id=chain(1), device_id_type=MESH)

    @pl.when(has_prev)
    def _():
        pl.semaphore_signal(barrier, inc=1, device_id=chain(-1), device_id_type=MESH)

    loads[3].wait()
    phase = jnp.int32(-1)
    for b in range(nb):
        for e in range(entries):
            entry = list_ref[b, e]
            distant = (entry >= 0) & (entry <= d * nb + b - LOCAL)
            phase = jnp.maximum(phase, jnp.where(distant, lax.rem(entry, STRIDE), -1))
    for b in range(nb):
        hit = lax.rem((d - 1) * nb + b + STRIDE, STRIDE) == phase
        wout[b : b + 1, :] = jnp.full((1, 128), jnp.where(hit, 1.0, 0.0), jnp.float32)
    if nb < wout.shape[0]:
        wout[nb:, :] = jnp.zeros((wout.shape[0] - nb, 128), jnp.float32)

    @pl.when(d == 0)
    def _():
        qpad[0:HALO, :] = jnp.zeros((HALO, qw), jnp.bfloat16)
        kvpad[:, 0:before, :] = jnp.zeros((2, before, kvw), jnp.bfloat16)

    @pl.when(d == last)
    def _():
        win[...] = jnp.zeros(win.shape, jnp.float32)

    fsum[...] = jnp.zeros(fsum.shape, jnp.bfloat16)

    w_copy = pltpu.make_async_remote_copy(
        wout, win, w_s, w_r, device_id=chain(-1), device_id_type=MESH
    )
    rim = pl.ds(tokens - HALO, HALO)
    body_rows = pl.ds(tokens - before, BLOCK)

    def to_next(src, dst, n):
        return pltpu.make_async_remote_copy(
            src, dst, tail_s.at[n], tail_r.at[n], device_id=chain(1), device_id_type=MESH
        )

    tails = [
        to_next(k_hbm.at[rim], kvpad.at[0, pl.ds(BLOCK, HALO)], 0),
        to_next(v_hbm.at[rim], kvpad.at[1, pl.ds(BLOCK, HALO)], 1),
        to_next(k_hbm.at[body_rows], kvpad.at[0, pl.ds(0, BLOCK)], 2),
        to_next(v_hbm.at[body_rows], kvpad.at[1, pl.ds(0, BLOCK)], 3),
        to_next(q_hbm.at[rim], qpad.at[pl.ds(0, HALO)], 4),
    ]

    def first_sends():
        pl.semaphore_wait(
            barrier,
            ni - 1 + no - 1 + jnp.where(has_next, 1, 0) + jnp.where(has_prev, 1, 0),
        )

        @pl.when(has_prev)
        def _():
            w_copy.start()

        @pl.when(has_next)
        def _():
            for copy in tails:
                copy.start()

    def kv_conv(b):
        rows = slice(b * BLOCK, b * BLOCK + before)
        dst = slice(b * BLOCK, (b + 1) * BLOCK)
        kvc[0, dst, :] = conv(kvpad[0, rows, :], kt_ref[...])
        kvc[1, dst, :] = conv(kvpad[1, rows, :], vt_ref[...])

    for n in (1, 5, 2, 6):
        loads[n].wait()
    for b in range(2, nb + 1):
        kv_conv(b)

    def candidate_step():
        @pl.when(has_prev)
        def _():
            tails[0].wait_recv()
            tails[1].wait_recv()

        kv_conv(1)

        @pl.when(has_next)
        def _():
            w_copy.wait_recv()

        for g in range(groups):
            cols = slice(g * HEAD_DIM, (g + 1) * HEAD_DIM)
            for half in range(2):
                total = jnp.zeros((BLOCK, HEAD_DIM), jnp.float32)
                for b in range(nb):
                    own = jnp.where(lax.rem(d * nb + b, STRIDE) == phase, 1.0, 0.0)
                    weight = jnp.maximum(win[b : b + 1, :], own)
                    rows = slice((b + 1) * BLOCK, (b + 2) * BLOCK)
                    total = total + weight * kvc[half, rows, cols].astype(jnp.float32)
                cand[half, :, cols] = total.astype(jnp.bfloat16)

        for half in range(2):
            for r in range(1, ni):
                scatter(half, r).start()

    def part(index):
        row = pl.multiple_of(index // col_parts * piece_rows, piece_rows)
        col = pl.multiple_of(lax.rem(index, col_parts) * piece_cols, piece_cols)
        return pl.ds(row, piece_rows), pl.ds(col, piece_cols)

    def scatter(half, r):
        return pltpu.make_async_remote_copy(
            cand.at[(half, *part(lax.rem(i + r, ni)))],
            rbuf.at[half, r],
            sc_s.at[half, r],
            sc_r.at[half, r],
            device_id=inner_peer(r),
            device_id_type=MESH,
        )

    def column(half, r):
        return pltpu.make_async_remote_copy(
            zpiece.at[half],
            zbuf.at[half, r],
            z_s.at[half, r],
            z_r.at[half, r],
            device_id={"outer": lax.rem(o + r, no)},
            device_id_type=MESH,
        )

    def gather(half, r):
        return pltpu.make_async_remote_copy(
            fsum.at[half],
            far.at[(half, slice(None), *part(i))],
            g_s.at[half, r],
            g_r.at[half, r],
            device_id=inner_peer(r),
            device_id_type=MESH,
        )

    def column_step(half):
        total = cand[(half, *part(i))].astype(jnp.float32)
        for r in range(1, ni):
            scatter(half, r).wait_recv()
            total = total + rbuf[half, r].astype(jnp.float32)
        zpiece[half] = total.astype(jnp.bfloat16)
        for r in range(1, no):
            pl.when(o + r < no)(column(half, r).start)

    def slot_of(row):
        return lax.rem(row * (ni * nb) // STRIDE, slots)

    def gather_step(half):
        fsum[half, slot_of(o)] = zpiece[half]
        for r in range(1, no):

            @pl.when(o >= r)
            def _():
                column(half, r).wait_recv()
                at = slot_of(o - r)
                fsum[half, at] = (
                    fsum[half, at].astype(jnp.float32) + zbuf[half, r].astype(jnp.float32)
                ).astype(jnp.bfloat16)

        for r in range(1, ni):
            gather(half, r).start()
        far[(half, slice(None), *part(i))] = fsum[half]

    def gather_wait(half):
        for r in range(1, ni):
            gather(half, r).wait_recv()

    loads[0].wait()
    loads[4].wait()

    row_ids = lax.broadcasted_iota(jnp.int32, (BLOCK, BLOCK), 0)
    col_ids = lax.broadcasted_iota(jnp.int32, (BLOCK, BLOCK), 1)
    causal = jnp.concatenate([row_ids >= col_ids] * per_group, 0)
    ones = jnp.ones((LOCAL * BLOCK, HEAD_DIM), jnp.bfloat16)

    def near(step, carry):
        b = jnp.where(step < nb - 2, step + 2, nb - 1 - step)

        @pl.when(b == 0)
        def _():
            @pl.when(has_prev)
            def _():
                tails[2].wait_recv()
                tails[3].wait_recv()
                tails[4].wait_recv()

            kv_conv(0)

        bias = jnp.where((b == 0) & (d == 0), NEG, 0.0)
        base = pl.multiple_of(b * BLOCK, BLOCK)
        for g in range(groups):
            wide = slice(g * per_group * HEAD_DIM, (g + 1) * per_group * HEAD_DIM)
            cols = slice(g * HEAD_DIM, (g + 1) * HEAD_DIM)
            q = conv(qpad[pl.ds(base, BLOCK + HALO), wide], qt_ref[:, wide])
            q = jnp.concatenate(
                [q[:, h * HEAD_DIM : (h + 1) * HEAD_DIM] for h in range(per_group)], 0
            )
            qs[b, g] = q
            k = kvc[0, pl.ds(base, LOCAL * BLOCK), cols]
            v = kvc[1, pl.ds(base, LOCAL * BLOCK), cols]
            s = lax.dot_general(q, k, NT, preferred_element_type=jnp.float32)
            prev = s[:, :BLOCK] + bias
            own = jnp.where(causal, s[:, BLOCK:], NEG)
            peak = jnp.max(jnp.maximum(prev, own), axis=1, keepdims=True)
            p = jnp.concatenate(
                [jnp.exp2((prev - peak) * SCALE), jnp.exp2((own - peak) * SCALE)], 1
            ).astype(jnp.bfloat16)
            acc_ref[b, g] = jnp.dot(
                p, jnp.concatenate([v, ones], 1), preferred_element_type=jnp.float32
            )
            max_ref[b, g] = jnp.broadcast_to(peak, (per_group * BLOCK, HEAD_DIM))

        pl.when(step == 0)(first_sends)
        pl.when(step == 1)(candidate_step)

        @pl.when(step == 2)
        def _():
            column_step(0)
            column_step(1)

        return carry

    lax.fori_loop(0, nb, near, 0)
    gather_step(0)
    gather_step(1)
    gather_wait(0)

    def distant_keys(b, carry):
        biases = []
        for n in range(slots):
            seen = jnp.int32(0)
            for e in range(entries):
                entry = list_ref[b, e]
                hit = (entry >= n * STRIDE) & (entry < (n + 1) * STRIDE)
                hit = hit & (entry <= d * nb + b - LOCAL)
                seen = jnp.where(hit, 1, seen)
            biases.append(jnp.where(seen > 0, 0.0, NEG))
        for g in range(groups):
            cols = slice(g * HEAD_DIM, (g + 1) * HEAD_DIM)
            q = qs[b, g]
            near_peak = max_ref[b, g]
            scores = []
            top = None
            for n in range(slots):
                s = lax.dot_general(q, far[0, n, :, cols], NT, preferred_element_type=jnp.float32)
                s = s + biases[n]
                scores.append(s)
                top = s if top is None else jnp.maximum(top, s)
            peak = jnp.maximum(near_peak, jnp.max(top, axis=1, keepdims=True))
            max_ref[b, g] = jnp.exp2((near_peak - peak) * SCALE)
            for n in range(slots):
                p = jnp.exp2((scores[n] - peak) * SCALE)
                pbuf[b, g, :, n * BLOCK : (n + 1) * BLOCK] = p.astype(jnp.bfloat16)
        return carry

    def distant_values(b, carry):
        base = pl.multiple_of(b * BLOCK, BLOCK)
        for g in range(groups):
            cols = slice(g * HEAD_DIM, (g + 1) * HEAD_DIM)
            both = acc_ref[b, g]
            shrink = max_ref[b, g]
            total = both[:, :HEAD_DIM] * shrink
            count = both[:, HEAD_DIM:] * shrink
            for n in range(slots):
                more = jnp.dot(
                    pbuf[b, g, :, n * BLOCK : (n + 1) * BLOCK],
                    jnp.concatenate([far[1, n, :, cols], ones[:BLOCK]], 1),
                    preferred_element_type=jnp.float32,
                )
                total = total + more[:, :HEAD_DIM]
                count = count + more[:, HEAD_DIM:]
            mixed = (total / count).astype(jnp.bfloat16)
            for h in range(per_group):
                head = g * per_group + h
                outb[pl.ds(base, BLOCK), head * HEAD_DIM : (head + 1) * HEAD_DIM] = mixed[
                    h * BLOCK : (h + 1) * BLOCK
                ]
        return carry

    lax.fori_loop(0, nb, distant_keys, 0)
    gather_wait(1)
    lax.fori_loop(0, nb, distant_values, 0)

    @pl.when(has_prev)
    def _():
        w_copy.wait_send()

    @pl.when(has_next)
    def _():
        for copy in tails:
            copy.wait_send()

    for half in range(2):
        for r in range(1, ni):
            scatter(half, r).wait_send()
            gather(half, r).wait_send()
        for r in range(1, no):
            pl.when(o + r < no)(column(half, r).wait_send)


def body(q_proj, k_proj, v_proj, q_taps, k_taps, v_taps, block_list):
    tokens, qw = q_proj.shape
    kvw = k_proj.shape[1]
    ni = lax.axis_size("inner")
    no = lax.axis_size("outer")
    nb = tokens // BLOCK
    groups = kvw // HEAD_DIM
    rows = qw // kvw * BLOCK
    slots = max(1, nb * ni * no // STRIDE)
    piece_rows = max(HALO, BLOCK // ni)
    piece_cols = BLOCK * kvw // (ni * piece_rows)
    piece = (piece_rows, piece_cols)
    dma = pltpu.SemaphoreType.DMA
    bf16, f32 = jnp.bfloat16, jnp.float32
    hbm_spec = pl.BlockSpec(memory_space=pltpu.HBM)
    scores = nb * groups * rows * (LOCAL + slots) * BLOCK
    return pl.pallas_call(
        functools.partial(kernel, ni, no),
        out_shape=jax.ShapeDtypeStruct((tokens, qw), bf16),
        in_specs=[hbm_spec] * 7,
        out_specs=pl.BlockSpec(memory_space=pltpu.VMEM),
        scratch_shapes=[
            pltpu.SMEM(block_list.shape, jnp.int32),
            pltpu.VMEM(q_taps.shape, f32),
            pltpu.VMEM(k_taps.shape, f32),
            pltpu.VMEM(v_taps.shape, f32),
            pltpu.VMEM((tokens + HALO, qw), bf16),
            pltpu.VMEM((2, tokens + BLOCK + HALO, kvw), bf16),
            pltpu.VMEM((2, tokens + BLOCK, kvw), bf16),
            pltpu.VMEM((nb, groups, rows, HEAD_DIM), bf16),
            pltpu.VMEM((nb, groups, rows, 2 * HEAD_DIM), f32),
            pltpu.VMEM((nb, groups, rows, HEAD_DIM), f32),
            pltpu.VMEM((nb, groups, rows, slots * BLOCK), bf16),
            pltpu.VMEM((max(8, nb), 128), f32),
            pltpu.VMEM((max(8, nb), 128), f32),
            pltpu.VMEM((2, BLOCK, kvw), bf16),
            pltpu.VMEM((2, ni, *piece), bf16),
            pltpu.VMEM((2, *piece), bf16),
            pltpu.VMEM((2, no, *piece), bf16),
            pltpu.VMEM((2, slots, *piece), bf16),
            pltpu.VMEM((2, slots, BLOCK, kvw), bf16),
            dma((7,)),
            dma((5,)),
            dma((5,)),
            dma,
            dma,
            dma((2, ni)),
            dma((2, ni)),
            dma((2, no)),
            dma((2, no)),
            dma((2, ni)),
            dma((2, ni)),
        ],
        compiler_params=pltpu.CompilerParams(
            collective_id=0, has_side_effects=True, vmem_limit_bytes=48 * 1024 * 1024
        ),
        cost_estimate=pl.CostEstimate(
            flops=4 * scores * HEAD_DIM,
            bytes_accessed=4 * tokens * qw + 4 * tokens * kvw,
            transcendentals=scores,
        ),
    )(*[pltpu.with_memory_space_constraint(x, pltpu.HBM) for x in (block_list, q_proj, k_proj, v_proj, q_taps, k_taps, v_taps)])


def solution(mesh):
    rows = P(("groups", "outer", "inner"), None)
    return jax.shard_map(
        body,
        mesh=mesh,
        in_specs=(rows, rows, rows, P(), P(), P(), rows),
        out_specs=rows,
        check_vma=False,
    )
```

profile of v0, /device:TPU:31, one launch (start us, length us, event | category | flops | bytes accessed | tf_op | source)
XLA Modules:
  0.0 24.7 jit_solution(5241176741107211604)
XLA Ops:
  0.0 23.3 %shard_map.73 = bf16[512,2048]{1,0:T(8,128)(2,1)S(1)} custom-call(s32[4,3]{1,0:T(4,128)} %list_hbm.1, bf16[512,2048]{1,0:T(8,128)(2,1)} %q_hbm.1, bf16[512,512]{1,0:T(8,128)(2,1)} %k_hbm.1, bf16[512,512]{1,0:T(8,128)(2,1)} %v_hbm.1, f32[3,2048]{1,0:T(4,128)} %qt_hbm.1, f32[3,512]{1,0:T(4,128)} %kt_hbm.1, f32[3,512]{1,0:T(4,128)} %vt_hbm.1), custom_call_target="tpu_custom_call" | custom-call | flops 1610612736 | bytes 5242880 | tf_op jit(solution)/shard_map/pallas_call | solution.py:400
  23.4 1.3 %copy.9 = bf16[512,2048]{1,0:T(8,128)(2,1)} copy(bf16[512,2048]{1,0:T(8,128)(2,1)S(1)} %shard_map.73) | data formatting | bytes 4194304
where the time goes:
time: 24.8 us; the launch traced here: 24.7 us
  Pallas kernels  23.3 us (94%)
  local copies, waits for them, and re-layouts  1.32 us (5%)
    pallas_call x1, Pallas kernels, body(): pl.pallas_call(functools.partial(kernel, ni, no), out_shape=jax.ShapeDtyp...  23.3 us
    unnamed x1, local copies, waits for them, and re-layouts  1.32 us

commit v1 on v0

--- a/solution.py
+++ b/solution.py
@@ -381,6 +381,520 @@
             pl.when(o + r < no)(column(half, r).wait_send)
 
 
+def paired_kernel(
+    no, list_hbm, q_hbm, k_hbm, v_hbm, qt_hbm, kt_hbm, vt_hbm, outb,
+    list_ref, qt_ref, kt_ref, vt_ref, qpad, kvpad, kvc, qs, acc_ref, max_ref, pbuf,
+    flag_out, flag_in, chip, cand, rrow, rprev, rsum, zrow, zfar, far,
+    in_sem, own_sem, fl_s, fl_r, raw_s, raw_r, rim_s, rim_r, tail_s, tail_r,
+    a_s, a_r, b_s, b_r, c_s, c_r, d_s, d_r, e_s, e_r,
+):
+    tokens, qw = q_hbm.shape
+    kvw = k_hbm.shape[1]
+    groups = kvw // HEAD_DIM
+    hw = kvw // 2
+    quarter = hw // 2
+    per_group = qw // kvw
+    nb = tokens // BLOCK
+    before = BLOCK + HALO
+    entries = list_ref.shape[1]
+    o = lax.axis_index("outer")
+    i = lax.axis_index("inner")
+    y = i // 2
+    c = lax.rem(i, 2)
+    m = o * 2 + y
+    last_chip = no * 2 - 1
+    d = o * 4 + i
+    has_next = d < 4 * no - 1
+    has_prev = d > 0
+    chip_next = m < last_chip
+    chip_prev = m > 0
+    first_core = c == 0
+    second_core = c == 1
+    odd = lax.rem(o, 2) == 1
+    even = lax.rem(o, 2) == 0
+
+    def chip_core(step, core):
+        other = m + step
+        return {"outer": other // 2, "inner": lax.rem(other, 2) * 2 + core}
+
+    def at(row, col):
+        return {"outer": row, "inner": col * 2 + c}
+
+    peer_core = {"inner": i + 1 - 2 * c}
+    peer_y = {"inner": lax.rem(i + 2, 4)}
+    next_device = {"outer": (d + 1) // 4, "inner": lax.rem(d + 1, 4)}
+
+    def greet(device):
+        pl.semaphore_signal(barrier, inc=1, device_id=device, device_id_type=MESH)
+
+    barrier = pltpu.get_barrier_semaphore()
+    greet(peer_core)
+    greet(peer_y)
+    pl.when(chip_next)(lambda: greet(chip_core(1, 0)))
+    pl.when(chip_prev)(lambda: greet(chip_core(-1, 1)))
+
+    @pl.when(odd)
+    def _():
+        greet(at(o - 1, 0))
+        greet(at(o - 1, 1))
+
+    for p in range(1, no, 2):
+
+        @pl.when(o > p)
+        def _():
+            greet(at(p, 0))
+            greet(at(p, 1))
+
+    loads = [
+        pltpu.make_async_copy(q_hbm, qpad.at[pl.ds(HALO, tokens)], in_sem.at[0]),
+        pltpu.make_async_copy(k_hbm, kvpad.at[0, pl.ds(before, tokens)], in_sem.at[1]),
+        pltpu.make_async_copy(v_hbm, kvpad.at[1, pl.ds(before, tokens)], in_sem.at[2]),
+        pltpu.make_async_copy(list_hbm, list_ref, in_sem.at[3]),
+        pltpu.make_async_copy(qt_hbm, qt_ref, in_sem.at[4]),
+        pltpu.make_async_copy(kt_hbm, kt_ref, in_sem.at[5]),
+        pltpu.make_async_copy(vt_hbm, vt_ref, in_sem.at[6]),
+    ]
+    half_cols = pl.ds(pl.multiple_of(c * hw, hw), hw)
+    peer_cols = pl.ds(pl.multiple_of((1 - c) * hw, hw), hw)
+    chip_rows = pl.ds(pl.multiple_of(HALO + c * tokens, HALO), tokens)
+    own = [
+        pltpu.make_async_copy(x.at[:, half_cols], chip.at[h, chip_rows], own_sem.at[h])
+        for h, x in enumerate((k_hbm, v_hbm))
+    ]
+    for n in (3, 1, 5, 2, 6, 0, 4):
+        loads[n].start()
+    for copy in own:
+        copy.start()
+
+    def remote(src, dst, send, recv, device):
+        return pltpu.make_async_remote_copy(
+            src, dst, send, recv, device_id=device, device_id_type=MESH
+        )
+
+    flag_back = [
+        remote(flag_out, flag_in.at[0], fl_s.at[k], fl_r.at[0], chip_core(-1, k)) for k in range(2)
+    ]
+    flag_peer = remote(flag_out, flag_in.at[1], fl_s.at[2], fl_r.at[1], peer_core)
+    raws = [
+        remote(x.at[:, peer_cols], chip.at[h, chip_rows], raw_s.at[h], raw_r.at[h], peer_core)
+        for h, x in enumerate((k_hbm, v_hbm))
+    ]
+    rim = pl.ds(tokens - HALO, HALO)
+    rims = [
+        [
+            remote(
+                x.at[rim, k * hw : (k + 1) * hw],
+                chip.at[h, pl.ds(0, HALO)],
+                rim_s.at[k, h],
+                rim_r.at[h],
+                chip_core(1, k),
+            )
+            for h, x in enumerate((k_hbm, v_hbm))
+        ]
+        for k in range(2)
+    ]
+    tail_rows = pl.ds(tokens - before, before)
+    tails = [
+        remote(k_hbm.at[tail_rows], kvpad.at[0, pl.ds(0, before)], tail_s.at[0], tail_r.at[0], next_device),
+        remote(v_hbm.at[tail_rows], kvpad.at[1, pl.ds(0, before)], tail_s.at[1], tail_r.at[1], next_device),
+        remote(q_hbm.at[rim], qpad.at[pl.ds(0, HALO)], tail_s.at[2], tail_r.at[2], next_device),
+    ]
+
+    @pl.when(jnp.logical_not(has_prev))
+    def _():
+        qpad[0:HALO, :] = jnp.zeros((HALO, qw), jnp.bfloat16)
+        kvpad[:, 0:before, :] = jnp.zeros((2, before, kvw), jnp.bfloat16)
+
+    @pl.when(jnp.logical_not(chip_prev))
+    def _():
+        chip[:, 0:HALO, :] = jnp.zeros((2, HALO, hw), jnp.bfloat16)
+
+    @pl.when(jnp.logical_not(chip_next))
+    def _():
+        flag_in[0] = jnp.full(flag_in.shape[1:], -1, jnp.int32)
+
+    @pl.when(second_core)
+    def _():
+        flag_in[1] = jnp.full(flag_in.shape[1:], -1, jnp.int32)
+
+    loads[3].wait()
+    phase = jnp.int32(-1)
+    for b in range(nb):
+        for e in range(entries):
+            entry = list_ref[b, e]
+            distant = (entry >= 0) & (entry <= d * nb + b - LOCAL)
+            phase = jnp.maximum(phase, jnp.where(distant, lax.rem(entry, STRIDE), -1))
+    flag_out[...] = jnp.full(flag_out.shape, phase, jnp.int32)
+
+    expected = 2 + jnp.where(first_core & chip_prev, 2, 0) + jnp.where(second_core & chip_next, 2, 0)
+    expected = expected + jnp.where(even, 2, 2 * (no - 1 - o))
+    pl.semaphore_wait(barrier, expected)
+
+    @pl.when(first_core & chip_prev)
+    def _():
+        for copy in flag_back:
+            copy.start()
+
+    @pl.when(second_core)
+    def _():
+        flag_peer.start()
+
+        @pl.when(chip_next)
+        def _():
+            for h in range(2):
+                for k in range(2):
+                    rims[k][h].start()
+
+    for copy in raws:
+        copy.start()
+
+    @pl.when(has_next)
+    def _():
+        for copy in tails:
+            copy.start()
+
+    def kv_conv(b):
+        rows = slice(b * BLOCK, b * BLOCK + before)
+        dst = slice(b * BLOCK, (b + 1) * BLOCK)
+        kvc[0, dst, :] = conv(kvpad[0, rows, :], kt_ref[...])
+        kvc[1, dst, :] = conv(kvpad[1, rows, :], vt_ref[...])
+
+    def cols_of(col):
+        return slice(col * quarter, (col + 1) * quarter)
+
+    def to_peer_site(h):
+        return remote(cand.at[h, 1 - y], rrow.at[h], a_s.at[h], a_r.at[h], peer_y)
+
+    def to_odd_row(h, col):
+        return remote(cand.at[h, col], rprev.at[h, y], b_s.at[h, col], b_r.at[h, y], at(o + 1, col))
+
+    def to_peer_col(h):
+        return remote(rsum.at[h], zrow.at[h], c_s.at[h], c_r.at[h], peer_y)
+
+    def to_later(h, row, col):
+        return remote(
+            rsum.at[h],
+            zfar.at[h, o // 2, y],
+            d_s.at[h, row, col],
+            d_r.at[h, o // 2, y],
+            at(row, col),
+        )
+
+    def from_earlier(h, p, col):
+        return remote(
+            rsum.at[h],
+            zfar.at[h, p, col],
+            d_s.at[h, 0, 0],
+            d_r.at[h, p, col],
+            peer_y,
+        )
+
+    def to_peer_core(h):
+        mine = pl.ds(2 * c, 2)
+        return remote(far.at[h, mine], far.at[h, mine], e_s.at[h], e_r.at[h], peer_core)
+
+    def from_peer_core(h):
+        theirs = pl.ds(2 - 2 * c, 2)
+        return remote(far.at[h, theirs], far.at[h, theirs], e_s.at[h], e_r.at[h], peer_core)
+
+    def candidate_step():
+        @pl.when(chip_next)
+        def _():
+            remote(flag_out, flag_in.at[0], fl_s.at[0], fl_r.at[0], peer_core).wait_recv()
+
+        @pl.when(first_core)
+        def _():
+            flag_peer.wait_recv()
+
+        known = jnp.maximum(jnp.maximum(flag_in[0, 0:1, :], flag_in[1, 0:1, :]), phase)
+        first = m * 2 * nb
+        weights = [
+            jnp.where(known == first + b, 1.0, 0.0).astype(jnp.bfloat16) for b in range(2 * nb)
+        ]
+        for h, taps in enumerate((kt_ref, vt_ref)):
+            own[h].wait()
+            raws[h].wait_recv()
+
+            @pl.when(chip_prev)
+            def _():
+                rims[0][h].wait_recv()
+
+            raw = weights[0] * chip[h, 0:before, :]
+            for b in range(1, 2 * nb):
+                raw = raw + weights[b] * chip[h, b * BLOCK : b * BLOCK + before, :]
+            total = conv(raw, taps[:, half_cols])
+            for col in range(2):
+                cand[h, col] = total[:, cols_of(col)]
+
+            @pl.when(even)
+            def _():
+                for col in range(2):
+                    to_odd_row(h, col).start()
+
+            to_peer_site(h).start()
+
+    def site_step(h):
+        to_peer_site(h).wait_recv()
+        rsum[h] = cand[h, y] + rrow[h]
+
+        @pl.when(odd)
+        def _():
+            for col in range(2):
+                remote(
+                    cand.at[h, col], rprev.at[h, col], b_s.at[h, col], b_r.at[h, col], peer_y
+                ).wait_recv()
+            rsum[h] = rsum[h] + rprev[h, 0] + rprev[h, 1]
+            for row in range(no - 1, 0, -1):
+
+                @pl.when(row > o)
+                def _():
+                    for col in range(2):
+                        to_later(h, row, col).start()
+
+        to_peer_col(h).start()
+
+    def final_step(h):
+        to_peer_col(h).wait_recv()
+        far[h, 2 * c + y] = rsum[h]
+        far[h, 2 * c + 1 - y] = zrow[h]
+        for p in range(no // 2):
+
+            @pl.when(o > 2 * p + 1)
+            def _():
+                for col in range(2):
+                    from_earlier(h, p, col).wait_recv()
+                    far[h, 2 * c + col] = far[h, 2 * c + col] + zfar[h, p, col]
+
+        to_peer_core(h).start()
+
+    for n in (1, 5, 2, 6):
+        loads[n].wait()
+    for b in range(2, nb + 1):
+        kv_conv(b)
+
+    loads[0].wait()
+    loads[4].wait()
+
+    row_ids = lax.broadcasted_iota(jnp.int32, (BLOCK, BLOCK), 0)
+    col_ids = lax.broadcasted_iota(jnp.int32, (BLOCK, BLOCK), 1)
+    causal = jnp.concatenate([row_ids >= col_ids] * per_group, 0)
+    ones = jnp.ones((LOCAL * BLOCK, HEAD_DIM), jnp.bfloat16)
+
+    def near(step, carry):
+        b = jnp.where(step < nb - 2, step + 2, nb - 1 - step)
+
+        @pl.when(b == 1)
+        def _():
+            @pl.when(has_prev)
+            def _():
+                tails[0].wait_recv()
+                tails[1].wait_recv()
+
+            kv_conv(1)
+
+        @pl.when(b == 0)
+        def _():
+            @pl.when(has_prev)
+            def _():
+                tails[2].wait_recv()
+
+            kv_conv(0)
+
+        bias = jnp.where((b == 0) & (d == 0), NEG, 0.0)
+        base = pl.multiple_of(b * BLOCK, BLOCK)
+        for g in range(groups):
+            wide = slice(g * per_group * HEAD_DIM, (g + 1) * per_group * HEAD_DIM)
+            cols = slice(g * HEAD_DIM, (g + 1) * HEAD_DIM)
+            q = conv(qpad[pl.ds(base, BLOCK + HALO), wide], qt_ref[:, wide])
+            q = jnp.concatenate(
+                [q[:, h * HEAD_DIM : (h + 1) * HEAD_DIM] for h in range(per_group)], 0
+            )
+            qs[b, g] = q
+            k = kvc[0, pl.ds(base, LOCAL * BLOCK), cols]
+            v = kvc[1, pl.ds(base, LOCAL * BLOCK), cols]
+            s = lax.dot_general(q, k, NT, preferred_element_type=jnp.float32)
+            prev = s[:, :BLOCK] + bias
+            mine = jnp.where(causal, s[:, BLOCK:], NEG)
+            peak = jnp.max(jnp.maximum(prev, mine), axis=1, keepdims=True)
+            p = jnp.concatenate(
+                [jnp.exp2((prev - peak) * SCALE), jnp.exp2((mine - peak) * SCALE)], 1
+            ).astype(jnp.bfloat16)
+            acc_ref[b, g] = jnp.dot(
+                p, jnp.concatenate([v, ones], 1), preferred_element_type=jnp.float32
+            )
+            max_ref[b, g] = jnp.broadcast_to(peak, (per_group * BLOCK, HEAD_DIM))
+            for at_step, at_group, run in HOOKS(candidate_step, site_step, final_step):
+                if at_group == g:
+                    pl.when(step == at_step)(run)
+
+        return carry
+
+    lax.fori_loop(0, nb, near, 0)
+    final_step(0)
+    final_step(1)
+    from_peer_core(0).wait_recv()
+
+    def distant_keys(b, carry):
+        seen = jnp.int32(0)
+        for e in range(entries):
+            entry = list_ref[b, e]
+            seen = jnp.where((entry >= 0) & (entry <= d * nb + b - LOCAL), 1, seen)
+        bias = jnp.where(seen > 0, 0.0, NEG)
+        for g in range(groups):
+            q = qs[b, g]
+            near_peak = max_ref[b, g]
+            s = lax.dot_general(q, far[0, g], NT, preferred_element_type=jnp.float32) + bias
+            peak = jnp.maximum(near_peak, jnp.max(s, axis=1, keepdims=True))
+            max_ref[b, g] = jnp.exp2((near_peak - peak) * SCALE)
+            pbuf[b, g] = jnp.exp2((s - peak) * SCALE).astype(jnp.bfloat16)
+        return carry
+
+    def distant_values(b, carry):
+        base = pl.multiple_of(b * BLOCK, BLOCK)
+        for g in range(groups):
+            both = acc_ref[b, g]
+            shrink = max_ref[b, g]
+            more = jnp.dot(
+                pbuf[b, g],
+                jnp.concatenate([far[1, g], ones[:BLOCK]], 1),
+                preferred_element_type=jnp.float32,
+            )
+            total = both[:, :HEAD_DIM] * shrink + more[:, :HEAD_DIM]
+            count = both[:, HEAD_DIM:] * shrink + more[:, HEAD_DIM:]
+            mixed = (total / count).astype(jnp.bfloat16)
+            for h in range(per_group):
+                head = g * per_group + h
+                outb[pl.ds(base, BLOCK), head * HEAD_DIM : (head + 1) * HEAD_DIM] = mixed[
+                    h * BLOCK : (h + 1) * BLOCK
+                ]
+        return carry
+
+    lax.fori_loop(0, nb, distant_keys, 0)
+    from_peer_core(1).wait_recv()
+    lax.fori_loop(0, nb, distant_values, 0)
+
+    @pl.when(first_core & chip_prev)
+    def _():
+        for copy in flag_back:
+            copy.wait_send()
+
+    @pl.when(second_core)
+    def _():
+        flag_peer.wait_send()
+
+        @pl.when(chip_next)
+        def _():
+            for k in range(2):
+                for copy in rims[k]:
+                    copy.wait_send()
+
+    @pl.when(has_next)
+    def _():
+        for copy in tails:
+            copy.wait_send()
+
+    for h in range(2):
+        raws[h].wait_send()
+        to_peer_site(h).wait_send()
+        to_peer_col(h).wait_send()
+        to_peer_core(h).wait_send()
+
+        @pl.when(even)
+        def _():
+            for col in range(2):
+                to_odd_row(h, col).wait_send()
+
+        @pl.when(odd)
+        def _():
+            for row in range(1, no):
+
+                @pl.when(row > o)
+                def _():
+                    for col in range(2):
+                        to_later(h, row, col).wait_send()
+
+
+def HOOKS(candidate_step, site_step, final_step):
+    return [
+        (0, 2, candidate_step),
+        (2, 2, lambda: site_step(0)),
+        (3, 1, lambda: site_step(1)),
+    ]
+
+
+def paired_call(arrays, no):
+    block_list, q_proj, k_proj = arrays[:3]
+    q_taps, k_taps, v_taps = arrays[4:]
+    tokens, qw = q_proj.shape
+    kvw = k_proj.shape[1]
+    nb = tokens // BLOCK
+    groups = kvw // HEAD_DIM
+    rows = qw // kvw * BLOCK
+    hw = kvw // 2
+    piece = (BLOCK, hw // 2)
+    dma = pltpu.SemaphoreType.DMA
+    bf16, f32 = jnp.bfloat16, jnp.float32
+    hbm_spec = pl.BlockSpec(memory_space=pltpu.HBM)
+    scores = nb * groups * rows * (LOCAL + 1) * BLOCK
+    return pl.pallas_call(
+        functools.partial(paired_kernel, no),
+        out_shape=jax.ShapeDtypeStruct((tokens, qw), bf16),
+        in_specs=[hbm_spec] * 7,
+        out_specs=pl.BlockSpec(memory_space=pltpu.VMEM),
+        scratch_shapes=[
+            pltpu.SMEM(block_list.shape, jnp.int32),
+            pltpu.VMEM(q_taps.shape, f32),
+            pltpu.VMEM(k_taps.shape, f32),
+            pltpu.VMEM(v_taps.shape, f32),
+            pltpu.VMEM((tokens + HALO, qw), bf16),
+            pltpu.VMEM((2, tokens + BLOCK + HALO, kvw), bf16),
+            pltpu.VMEM((2, tokens + BLOCK, kvw), bf16),
+            pltpu.VMEM((nb, groups, rows, HEAD_DIM), bf16),
+            pltpu.VMEM((nb, groups, rows, 2 * HEAD_DIM), f32),
+            pltpu.VMEM((nb, groups, rows, HEAD_DIM), f32),
+            pltpu.VMEM((nb, groups, rows, BLOCK), bf16),
+            pltpu.VMEM((8, hw), jnp.int32),
+            pltpu.VMEM((2, 8, hw), jnp.int32),
+            pltpu.VMEM((2, 2 * tokens + HALO, hw), bf16),
+            pltpu.VMEM((2, 2, *piece), bf16),
+            pltpu.VMEM((2, *piece), bf16),
+            pltpu.VMEM((2, 2, *piece), bf16),
+            pltpu.VMEM((2, *piece), bf16),
+            pltpu.VMEM((2, *piece), bf16),
+            pltpu.VMEM((2, no // 2, 2, *piece), bf16),
+            pltpu.VMEM((2, groups, BLOCK, HEAD_DIM), bf16),
+            dma((7,)),
+            dma((2,)),
+            dma((3,)),
+            dma((2,)),
+            dma((2,)),
+            dma((2,)),
+            dma((2, 2)),
+            dma((2,)),
+            dma((3,)),
+            dma((3,)),
+            dma((2,)),
+            dma((2,)),
+            dma((2, 2)),
+            dma((2, 2)),
+            dma((2,)),
+            dma((2,)),
+            dma((2, no, 2)),
+            dma((2, no // 2, 2)),
+            dma((2,)),
+            dma((2,)),
+        ],
+        compiler_params=pltpu.CompilerParams(
+            collective_id=0, has_side_effects=True, vmem_limit_bytes=48 * 1024 * 1024
+        ),
+        cost_estimate=pl.CostEstimate(
+            flops=4 * scores * HEAD_DIM,
+            bytes_accessed=4 * tokens * qw + 4 * tokens * kvw,
+            transcendentals=scores,
+        ),
+    )(*arrays)
+
+
 def body(q_proj, k_proj, v_proj, q_taps, k_taps, v_taps, block_list):
     tokens, qw = q_proj.shape
     kvw = k_proj.shape[1]
@@ -397,6 +911,13 @@
     bf16, f32 = jnp.bfloat16, jnp.float32
     hbm_spec = pl.BlockSpec(memory_space=pltpu.HBM)
     scores = nb * groups * rows * (LOCAL + slots) * BLOCK
+    arrays = [
+        pltpu.with_memory_space_constraint(x, pltpu.HBM)
+        for x in (block_list, q_proj, k_proj, v_proj, q_taps, k_taps, v_taps)
+    ]
+    paired = ni == 4 and no % 2 == 0 and nb * ni * no == STRIDE and groups == 4 and nb >= 2
+    if paired:
+        return paired_call(arrays, no)
     return pl.pallas_call(
         functools.partial(kernel, ni, no),
         out_shape=jax.ShapeDtypeStruct((tokens, qw), bf16),
@@ -442,7 +963,7 @@
             bytes_accessed=4 * tokens * qw + 4 * tokens * kvw,
             transcendentals=scores,
         ),
-    )(*[pltpu.with_memory_space_constraint(x, pltpu.HBM) for x in (block_list, q_proj, k_proj, v_proj, q_taps, k_taps, v_taps)])
+    )(*arrays)
 
 
 def solution(mesh):

time: 24.8 us -> 24.9 us (level)
  the two profiles are of different devices: /device:TPU:31 before, /device:TPU:16 now
where the time goes in v1:
time: 24.9 us; the launch traced here: 24.8 us
  Pallas kernels  23.5 us (94%)
  local copies, waits for them, and re-layouts  1.32 us (5%)
    pallas_call x1, Pallas kernels, paired_call(): pl.pallas_call(functools.partial(paired_kernel, no), out_shape=jax.ShapeD...  23.5 us
    unnamed x1, local copies, waits for them, and re-layouts  1.32 us

profile of v1, /device:TPU:16, one launch (start us, length us, event | category | flops | bytes accessed | tf_op | source)
XLA Modules:
  0.0 24.8 jit_solution(9851069845800688211)
XLA Ops:
  0.0 23.5 %shard_map.73 = bf16[512,2048]{1,0:T(8,128)(2,1)S(1)} custom-call(s32[4,3]{1,0:T(4,128)} %list_hbm.1, bf16[512,2048]{1,0:T(8,128)(2,1)} %q_hbm.1, bf16[512,512]{1,0:T(8,128)(2,1)} %k_hbm.1, bf16[512,512]{1,0:T(8,128)(2,1)} %v_hbm.1, f32[3,2048]{1,0:T(4,128)} %qt_hbm.1, f32[3,512]{1,0:T(4,128)} %kt_hbm.1, f32[3,512]{1,0:T(4,128)} %vt_hbm.1), custom_call_target="tpu_custom_call" | custom-call | flops 1610612736 | bytes 5242880 | tf_op jit(solution)/shard_map/pallas_call | solution.py:839
  23.5 1.3 %copy.9 = bf16[512,2048]{1,0:T(8,128)(2,1)} copy(bf16[512,2048]{1,0:T(8,128)(2,1)S(1)} %shard_map.73) | data formatting | bytes 4194304

commit v2 on v1

--- a/solution.py
+++ b/solution.py
@@ -381,12 +381,27 @@
             pl.when(o + r < no)(column(half, r).wait_send)
 
 
+ROWS = 4
+SUMS = ({0: (1,), 2: (3,)}, {0: (1, 2), 1: (2,)})
+SPREADS = ({1: (3, 2)}, {2: (3,)})
+SITE_STEPS = ((2, 2), (3, 3))
+TAILS_EARLY = True
+
+
+def dests(row):
+    return sorted({r for table in (*SUMS, *SPREADS) for r in table.get(row, ())})
+
+
+def origins(row):
+    return sorted({s for table in (*SUMS, *SPREADS) for s, rows in table.items() if row in rows})
+
+
 def paired_kernel(
-    no, list_hbm, q_hbm, k_hbm, v_hbm, qt_hbm, kt_hbm, vt_hbm, outb,
+    list_hbm, q_hbm, k_hbm, v_hbm, qt_hbm, kt_hbm, vt_hbm, outb,
     list_ref, qt_ref, kt_ref, vt_ref, qpad, kvpad, kvc, qs, acc_ref, max_ref, pbuf,
-    flag_out, flag_in, chip, cand, rrow, rprev, rsum, zrow, zfar, far,
+    flag_out, flag_in, chip, cand, rrow, rother, rsum, zrow, zfar, far,
     in_sem, own_sem, fl_s, fl_r, raw_s, raw_r, rim_s, rim_r, tail_s, tail_r,
-    a_s, a_r, b_s, b_r, c_s, c_r, d_s, d_r, e_s, e_r,
+    a_s, a_r, b_s, b_r, c_s, c_r, d_s, d_r, e_s, e_r, ready,
 ):
     tokens, qw = q_hbm.shape
     kvw = k_hbm.shape[1]
@@ -402,6 +417,7 @@
     y = i // 2
     c = lax.rem(i, 2)
     m = o * 2 + y
+    no = ROWS
     last_chip = no * 2 - 1
     d = o * 4 + i
     has_next = d < 4 * no - 1
@@ -410,8 +426,6 @@
     chip_prev = m > 0
     first_core = c == 0
     second_core = c == 1
-    odd = lax.rem(o, 2) == 1
-    even = lax.rem(o, 2) == 0
 
     def chip_core(step, core):
         other = m + step
@@ -424,26 +438,13 @@
     peer_y = {"inner": lax.rem(i + 2, 4)}
     next_device = {"outer": (d + 1) // 4, "inner": lax.rem(d + 1, 4)}
 
+    barrier = pltpu.get_barrier_semaphore()
+
     def greet(device):
         pl.semaphore_signal(barrier, inc=1, device_id=device, device_id_type=MESH)
 
-    barrier = pltpu.get_barrier_semaphore()
-    greet(peer_core)
-    greet(peer_y)
-    pl.when(chip_next)(lambda: greet(chip_core(1, 0)))
-    pl.when(chip_prev)(lambda: greet(chip_core(-1, 1)))
-
-    @pl.when(odd)
-    def _():
-        greet(at(o - 1, 0))
-        greet(at(o - 1, 1))
-
-    for p in range(1, no, 2):
-
-        @pl.when(o > p)
-        def _():
-            greet(at(p, 0))
-            greet(at(p, 1))
+    def call(device):
+        pl.semaphore_signal(ready, inc=1, device_id=device, device_id_type=MESH)
 
     loads = [
         pltpu.make_async_copy(q_hbm, qpad.at[pl.ds(HALO, tokens)], in_sem.at[0]),
@@ -461,10 +462,30 @@
         pltpu.make_async_copy(x.at[:, half_cols], chip.at[h, chip_rows], own_sem.at[h])
         for h, x in enumerate((k_hbm, v_hbm))
     ]
-    for n in (3, 1, 5, 2, 6, 0, 4):
+    loads[3].start()
+    greet(peer_core)
+    greet(peer_y)
+
+    @pl.when(chip_next)
+    def _():
+        greet(chip_core(1, 0))
+        pl.when(second_core)(lambda: greet(chip_core(1, 1)))
+
+    for row in range(no):
+        if dests(row):
+
+            @pl.when(o == row)
+            def _():
+                for dst in dests(row):
+                    greet(at(dst, 0))
+                    greet(at(dst, 1))
+
+    for n in (1, 5, 2, 6):
         loads[n].start()
     for copy in own:
         copy.start()
+    for n in (0, 4):
+        loads[n].start()
 
     def remote(src, dst, send, recv, device):
         return pltpu.make_async_remote_copy(
@@ -517,6 +538,25 @@
     def _():
         flag_in[1] = jnp.full(flag_in.shape[1:], -1, jnp.int32)
 
+    expected = 2 + jnp.where(chip_prev, jnp.where(first_core, 2, 1), 0)
+    awaited = jnp.where(second_core & chip_next, 2, 0)
+    for row in range(no):
+        expected = expected + jnp.where(o == row, 2 * len(origins(row)), 0)
+        awaited = awaited + jnp.where(o == row, 2 * len(dests(row)), 0)
+    pl.semaphore_wait(barrier, expected)
+    pl.when(chip_prev)(lambda: call(chip_core(-1, 1)))
+    for row in range(no):
+        if origins(row):
+
+            @pl.when(o == row)
+            def _():
+                for src in origins(row):
+                    call(at(src, 0))
+                    call(at(src, 1))
+
+    for copy in raws:
+        copy.start()
+
     loads[3].wait()
     phase = jnp.int32(-1)
     for b in range(nb):
@@ -526,32 +566,28 @@
             phase = jnp.maximum(phase, jnp.where(distant, lax.rem(entry, STRIDE), -1))
     flag_out[...] = jnp.full(flag_out.shape, phase, jnp.int32)
 
-    expected = 2 + jnp.where(first_core & chip_prev, 2, 0) + jnp.where(second_core & chip_next, 2, 0)
-    expected = expected + jnp.where(even, 2, 2 * (no - 1 - o))
-    pl.semaphore_wait(barrier, expected)
-
     @pl.when(first_core & chip_prev)
     def _():
         for copy in flag_back:
             copy.start()
 
-    @pl.when(second_core)
-    def _():
-        flag_peer.start()
-
-        @pl.when(chip_next)
-        def _():
-            for h in range(2):
-                for k in range(2):
-                    rims[k][h].start()
-
-    for copy in raws:
-        copy.start()
-
-    @pl.when(has_next)
-    def _():
-        for copy in tails:
-            copy.start()
+    pl.when(second_core)(flag_peer.start)
+    pl.when(awaited > 0)(lambda: pl.semaphore_wait(ready, awaited))
+
+    @pl.when(second_core & chip_next)
+    def _():
+        for h in range(2):
+            for k in range(2):
+                rims[k][h].start()
+
+    def tail_sends():
+        @pl.when(has_next)
+        def _():
+            for copy in tails:
+                copy.start()
+
+    if TAILS_EARLY:
+        tail_sends()
 
     def kv_conv(b):
         rows = slice(b * BLOCK, b * BLOCK + before)
@@ -565,28 +601,27 @@
     def to_peer_site(h):
         return remote(cand.at[h, 1 - y], rrow.at[h], a_s.at[h], a_r.at[h], peer_y)
 
-    def to_odd_row(h, col):
-        return remote(cand.at[h, col], rprev.at[h, y], b_s.at[h, col], b_r.at[h, y], at(o + 1, col))
+    def to_site(h, row, col):
+        return remote(
+            cand.at[h, col], rother.at[h, o, y], b_s.at[h, row, col], b_r.at[h, o, y], at(row, col)
+        )
+
+    def at_site(h, src, col):
+        return remote(
+            cand.at[h, col], rother.at[h, src, col], b_s.at[h, 0, col], b_r.at[h, src, col], peer_y
+        )
 
     def to_peer_col(h):
         return remote(rsum.at[h], zrow.at[h], c_s.at[h], c_r.at[h], peer_y)
 
     def to_later(h, row, col):
         return remote(
-            rsum.at[h],
-            zfar.at[h, o // 2, y],
-            d_s.at[h, row, col],
-            d_r.at[h, o // 2, y],
-            at(row, col),
+            rsum.at[h], zfar.at[h, o, y], d_s.at[h, row, col], d_r.at[h, o, y], at(row, col)
         )
 
-    def from_earlier(h, p, col):
+    def from_earlier(h, src, col):
         return remote(
-            rsum.at[h],
-            zfar.at[h, p, col],
-            d_s.at[h, 0, 0],
-            d_r.at[h, p, col],
-            peer_y,
+            rsum.at[h], zfar.at[h, src, col], d_s.at[h, 0, 0], d_r.at[h, src, col], peer_y
         )
 
     def to_peer_core(h):
@@ -626,28 +661,38 @@
             for col in range(2):
                 cand[h, col] = total[:, cols_of(col)]
 
-            @pl.when(even)
-            def _():
-                for col in range(2):
-                    to_odd_row(h, col).start()
+            for src, rows in SUMS[h].items():
+
+                @pl.when(o == src)
+                def _():
+                    for row in rows:
+                        for col in range(2):
+                            to_site(h, row, col).start()
 
             to_peer_site(h).start()
+
+        if not TAILS_EARLY:
+            tail_sends()
 
     def site_step(h):
         to_peer_site(h).wait_recv()
         rsum[h] = cand[h, y] + rrow[h]
-
-        @pl.when(odd)
-        def _():
-            for col in range(2):
-                remote(
-                    cand.at[h, col], rprev.at[h, col], b_s.at[h, col], b_r.at[h, col], peer_y
-                ).wait_recv()
-            rsum[h] = rsum[h] + rprev[h, 0] + rprev[h, 1]
-            for row in range(no - 1, 0, -1):
-
-                @pl.when(row > o)
+        for row in range(no):
+            sources = [src for src, rows in SUMS[h].items() if row in rows]
+            if sources:
+
+                @pl.when(o == row)
                 def _():
+                    for src in sources:
+                        for col in range(2):
+                            at_site(h, src, col).wait_recv()
+                            rsum[h] = rsum[h] + rother[h, src, col]
+
+        for src, rows in SPREADS[h].items():
+
+            @pl.when(o == src)
+            def _():
+                for row in rows:
                     for col in range(2):
                         to_later(h, row, col).start()
 
@@ -657,13 +702,14 @@
         to_peer_col(h).wait_recv()
         far[h, 2 * c + y] = rsum[h]
         far[h, 2 * c + 1 - y] = zrow[h]
-        for p in range(no // 2):
-
-            @pl.when(o > 2 * p + 1)
-            def _():
-                for col in range(2):
-                    from_earlier(h, p, col).wait_recv()
-                    far[h, 2 * c + col] = far[h, 2 * c + col] + zfar[h, p, col]
+        for src, rows in SPREADS[h].items():
+            for row in rows:
+
+                @pl.when(o == row)
+                def _():
+                    for col in range(2):
+                        from_earlier(h, src, col).wait_recv()
+                        far[h, 2 * c + col] = far[h, 2 * c + col] + zfar[h, src, col]
 
         to_peer_core(h).start()
 
@@ -671,6 +717,7 @@
         loads[n].wait()
     for b in range(2, nb + 1):
         kv_conv(b)
+    candidate_step()
 
     loads[0].wait()
     loads[4].wait()
@@ -723,24 +770,23 @@
                 p, jnp.concatenate([v, ones], 1), preferred_element_type=jnp.float32
             )
             max_ref[b, g] = jnp.broadcast_to(peak, (per_group * BLOCK, HEAD_DIM))
-            for at_step, at_group, run in HOOKS(candidate_step, site_step, final_step):
+            for (at_step, at_group), h in zip(SITE_STEPS, range(2)):
                 if at_group == g:
-                    pl.when(step == at_step)(run)
+                    pl.when(step == at_step)(functools.partial(site_step, h))
 
         return carry
 
     lax.fori_loop(0, nb, near, 0)
     final_step(0)
-    final_step(1)
-    from_peer_core(0).wait_recv()
-
-    def distant_keys(b, carry):
+
+    def distant_keys(first, b, carry):
         seen = jnp.int32(0)
         for e in range(entries):
             entry = list_ref[b, e]
             seen = jnp.where((entry >= 0) & (entry <= d * nb + b - LOCAL), 1, seen)
         bias = jnp.where(seen > 0, 0.0, NEG)
-        for g in range(groups):
+        for n in range(2):
+            g = first + n
             q = qs[b, g]
             near_peak = max_ref[b, g]
             s = lax.dot_general(q, far[0, g], NT, preferred_element_type=jnp.float32) + bias
@@ -749,9 +795,10 @@
             pbuf[b, g] = jnp.exp2((s - peak) * SCALE).astype(jnp.bfloat16)
         return carry
 
-    def distant_values(b, carry):
+    def distant_values(first, b, carry):
         base = pl.multiple_of(b * BLOCK, BLOCK)
-        for g in range(groups):
+        for n in range(2):
+            g = first + n
             both = acc_ref[b, g]
             shrink = max_ref[b, g]
             more = jnp.dot(
@@ -763,15 +810,21 @@
             count = both[:, HEAD_DIM:] * shrink + more[:, HEAD_DIM:]
             mixed = (total / count).astype(jnp.bfloat16)
             for h in range(per_group):
-                head = g * per_group + h
-                outb[pl.ds(base, BLOCK), head * HEAD_DIM : (head + 1) * HEAD_DIM] = mixed[
+                col = pl.multiple_of((g * per_group + h) * HEAD_DIM, HEAD_DIM)
+                outb[pl.ds(base, BLOCK), pl.ds(col, HEAD_DIM)] = mixed[
                     h * BLOCK : (h + 1) * BLOCK
                 ]
         return carry
 
-    lax.fori_loop(0, nb, distant_keys, 0)
+    mine = 2 * c
+    theirs = 2 - 2 * c
+    lax.fori_loop(0, nb, functools.partial(distant_keys, mine), 0, unroll=2)
+    from_peer_core(0).wait_recv()
+    lax.fori_loop(0, nb, functools.partial(distant_keys, theirs), 0, unroll=2)
+    final_step(1)
+    lax.fori_loop(0, nb, functools.partial(distant_values, mine), 0, unroll=2)
     from_peer_core(1).wait_recv()
-    lax.fori_loop(0, nb, distant_values, 0)
+    lax.fori_loop(0, nb, functools.partial(distant_values, theirs), 0, unroll=2)
 
     @pl.when(first_core & chip_prev)
     def _():
@@ -799,30 +852,17 @@
         to_peer_col(h).wait_send()
         to_peer_core(h).wait_send()
 
-        @pl.when(even)
-        def _():
-            for col in range(2):
-                to_odd_row(h, col).wait_send()
-
-        @pl.when(odd)
-        def _():
-            for row in range(1, no):
-
-                @pl.when(row > o)
+        for table, copy in ((SUMS, to_site), (SPREADS, to_later)):
+            for src, rows in table[h].items():
+
+                @pl.when(o == src)
                 def _():
-                    for col in range(2):
-                        to_later(h, row, col).wait_send()
-
-
-def HOOKS(candidate_step, site_step, final_step):
-    return [
-        (0, 2, candidate_step),
-        (2, 2, lambda: site_step(0)),
-        (3, 1, lambda: site_step(1)),
-    ]
-
-
-def paired_call(arrays, no):
+                    for row in rows:
+                        for col in range(2):
+                            copy(h, row, col).wait_send()
+
+
+def paired_call(arrays):
     block_list, q_proj, k_proj = arrays[:3]
     q_taps, k_taps, v_taps = arrays[4:]
     tokens, qw = q_proj.shape
@@ -837,7 +877,7 @@
     hbm_spec = pl.BlockSpec(memory_space=pltpu.HBM)
     scores = nb * groups * rows * (LOCAL + 1) * BLOCK
     return pl.pallas_call(
-        functools.partial(paired_kernel, no),
+        paired_kernel,
         out_shape=jax.ShapeDtypeStruct((tokens, qw), bf16),
         in_specs=[hbm_spec] * 7,
         out_specs=pl.BlockSpec(memory_space=pltpu.VMEM),
@@ -858,10 +898,10 @@
             pltpu.VMEM((2, 2 * tokens + HALO, hw), bf16),
             pltpu.VMEM((2, 2, *piece), bf16),
             pltpu.VMEM((2, *piece), bf16),
-            pltpu.VMEM((2, 2, *piece), bf16),
+            pltpu.VMEM((2, ROWS, 2, *piece), bf16),
             pltpu.VMEM((2, *piece), bf16),
             pltpu.VMEM((2, *piece), bf16),
-            pltpu.VMEM((2, no // 2, 2, *piece), bf16),
+            pltpu.VMEM((2, ROWS, 2, *piece), bf16),
             pltpu.VMEM((2, groups, BLOCK, HEAD_DIM), bf16),
             dma((7,)),
             dma((2,)),
@@ -875,14 +915,15 @@
             dma((3,)),
             dma((2,)),
             dma((2,)),
-            dma((2, 2)),
-            dma((2, 2)),
+            dma((2, ROWS, 2)),
+            dma((2, ROWS, 2)),
             dma((2,)),
             dma((2,)),
-            dma((2, no, 2)),
-            dma((2, no // 2, 2)),
+            dma((2, ROWS, 2)),
+            dma((2, ROWS, 2)),
             dma((2,)),
             dma((2,)),
+            pltpu.SemaphoreType.REGULAR,
         ],
         compiler_params=pltpu.CompilerParams(
             collective_id=0, has_side_effects=True, vmem_limit_bytes=48 * 1024 * 1024
@@ -915,9 +956,9 @@
         pltpu.with_memory_space_constraint(x, pltpu.HBM)
         for x in (block_list, q_proj, k_proj, v_proj, q_taps, k_taps, v_taps)
     ]
-    paired = ni == 4 and no % 2 == 0 and nb * ni * no == STRIDE and groups == 4 and nb >= 2
+    paired = ni == 4 and no == ROWS and nb * ni * no == STRIDE and groups == 4 and nb >= 2
     if paired:
-        return paired_call(arrays, no)
+        return paired_call(arrays)
     return pl.pallas_call(
         functools.partial(kernel, ni, no),
         out_shape=jax.ShapeDtypeStruct((tokens, qw), bf16),

time: 24.9 us -> 23.8 us (0.956)
  the two profiles are of different devices: /device:TPU:16 before, /device:TPU:17 now
where the time goes in v2:
time: 23.8 us; the launch traced here: 23.7 us
  Pallas kernels  22.4 us (94%)
  local copies, waits for them, and re-layouts  1.32 us (6%)
    pallas_call x1, Pallas kernels, paired_call(): pl.pallas_call(paired_kernel, out_shape=jax.ShapeDtypeStruct((tokens, qw)...  22.4 us
    unnamed x1, local copies, waits for them, and re-layouts  1.32 us

profile of v2, /device:TPU:17, one launch (start us, length us, event | category | flops | bytes accessed | tf_op | source)
XLA Modules:
  0.0 23.7 jit_solution(16305847368233484824)
XLA Ops:
  0.0 22.4 %shard_map.73 = bf16[512,2048]{1,0:T(8,128)(2,1)S(1)} custom-call(s32[4,3]{1,0:T(4,128)} %list_hbm.1, bf16[512,2048]{1,0:T(8,128)(2,1)} %q_hbm.1, bf16[512,512]{1,0:T(8,128)(2,1)} %k_hbm.1, bf16[512,512]{1,0:T(8,128)(2,1)} %v_hbm.1, f32[3,2048]{1,0:T(4,128)} %qt_hbm.1, f32[3,512]{1,0:T(4,128)} %kt_hbm.1, f32[3,512]{1,0:T(4,128)} %vt_hbm.1), custom_call_target="tpu_custom_call" | custom-call | flops 1610612736 | bytes 5242880 | tf_op jit(solution)/shard_map/pallas_call | solution.py:879
  22.4 1.3 %copy.9 = bf16[512,2048]{1,0:T(8,128)(2,1)} copy(bf16[512,2048]{1,0:T(8,128)(2,1)S(1)} %shard_map.73) | data formatting | bytes 4194304

commit v3 on v2

--- a/solution.py
+++ b/solution.py
@@ -382,18 +382,19 @@
 
 
 ROWS = 4
-SUMS = ({0: (1,), 2: (3,)}, {0: (1, 2), 1: (2,)})
+SUMS = ({0: (1,), 2: (3,)}, {0: (2, 1), 1: (2,)})
 SPREADS = ({1: (3, 2)}, {2: (3,)})
 SITE_STEPS = ((2, 2), (3, 3))
-TAILS_EARLY = True
-
-
-def dests(row):
-    return sorted({r for table in (*SUMS, *SPREADS) for r in table.get(row, ())})
-
-
-def origins(row):
-    return sorted({s for table in (*SUMS, *SPREADS) for s, rows in table.items() if row in rows})
+LATE = ((2, 3), (1, 3), (0, 2))
+
+
+def dests(row, late):
+    rows = {r for table in (*SUMS, *SPREADS) for r in table.get(row, ())}
+    return sorted(r for r in rows if ((row, r) in LATE) == late)
+
+
+def origins(row, late):
+    return [r for r in range(ROWS) if row in dests(r, late)]
 
 
 def paired_kernel(
@@ -466,19 +467,26 @@
     greet(peer_core)
     greet(peer_y)
 
+    late_next = (y == 1) & functools.reduce(
+        jnp.logical_or, [o == row for row in range(no - 1) if (row, row + 1) in LATE]
+    )
+    late_prev = (y == 0) & functools.reduce(
+        jnp.logical_or, [o == row + 1 for row in range(no - 1) if (row, row + 1) in LATE]
+    )
+
     @pl.when(chip_next)
     def _():
         greet(chip_core(1, 0))
-        pl.when(second_core)(lambda: greet(chip_core(1, 1)))
-
+        pl.when(second_core & late_next)(lambda: greet(chip_core(1, 1)))
+
+    pl.when(chip_prev & jnp.logical_not(late_prev))(lambda: greet(chip_core(-1, 1)))
     for row in range(no):
-        if dests(row):
-
-            @pl.when(o == row)
-            def _():
-                for dst in dests(row):
-                    greet(at(dst, 0))
-                    greet(at(dst, 1))
+
+        @pl.when(o == row)
+        def _():
+            for other in origins(row, False) + dests(row, True):
+                greet(at(other, 0))
+                greet(at(other, 1))
 
     for n in (1, 5, 2, 6):
         loads[n].start()
@@ -538,19 +546,23 @@
     def _():
         flag_in[1] = jnp.full(flag_in.shape[1:], -1, jnp.int32)
 
-    expected = 2 + jnp.where(chip_prev, jnp.where(first_core, 2, 1), 0)
-    awaited = jnp.where(second_core & chip_next, 2, 0)
+    expected = 2 + jnp.where(chip_prev & first_core, 2, 0)
+    expected = expected + jnp.where(chip_prev & late_prev & second_core, 1, 0)
+    sends_on = second_core & chip_next
+    expected = expected + jnp.where(sends_on & jnp.logical_not(late_next), 2, 0)
+    awaited = jnp.where(sends_on & late_next, 2, 0)
     for row in range(no):
-        expected = expected + jnp.where(o == row, 2 * len(origins(row)), 0)
-        awaited = awaited + jnp.where(o == row, 2 * len(dests(row)), 0)
+        met = 2 * len(dests(row, False) + origins(row, True))
+        expected = expected + jnp.where(o == row, met, 0)
+        awaited = awaited + jnp.where(o == row, 2 * len(dests(row, True)), 0)
     pl.semaphore_wait(barrier, expected)
-    pl.when(chip_prev)(lambda: call(chip_core(-1, 1)))
+    pl.when(chip_prev & late_prev)(lambda: call(chip_core(-1, 1)))
     for row in range(no):
-        if origins(row):
+        if origins(row, True):
 
             @pl.when(o == row)
             def _():
-                for src in origins(row):
+                for src in origins(row, True):
                     call(at(src, 0))
                     call(at(src, 1))
 
@@ -572,22 +584,20 @@
             copy.start()
 
     pl.when(second_core)(flag_peer.start)
-    pl.when(awaited > 0)(lambda: pl.semaphore_wait(ready, awaited))
-
-    @pl.when(second_core & chip_next)
-    def _():
-        for h in range(2):
-            for k in range(2):
-                rims[k][h].start()
-
-    def tail_sends():
+    def next_sends():
+        @pl.when(sends_on)
+        def _():
+            for h in range(2):
+                for k in range(2):
+                    rims[k][h].start()
+
         @pl.when(has_next)
         def _():
             for copy in tails:
                 copy.start()
 
-    if TAILS_EARLY:
-        tail_sends()
+    held_back = sends_on & late_next
+    pl.when(jnp.logical_not(held_back))(next_sends)
 
     def kv_conv(b):
         rows = slice(b * BLOCK, b * BLOCK + before)
@@ -633,6 +643,9 @@
         return remote(far.at[h, theirs], far.at[h, theirs], e_s.at[h], e_r.at[h], peer_core)
 
     def candidate_step():
+        pl.when(awaited > 0)(lambda: pl.semaphore_wait(ready, awaited))
+        pl.when(held_back)(next_sends)
+
         @pl.when(chip_next)
         def _():
             remote(flag_out, flag_in.at[0], fl_s.at[0], fl_r.at[0], peer_core).wait_recv()
@@ -670,9 +683,6 @@
                             to_site(h, row, col).start()
 
             to_peer_site(h).start()
-
-        if not TAILS_EARLY:
-            tail_sends()
 
     def site_step(h):
         to_peer_site(h).wait_recv()

time: 23.8 us -> 22.6 us (0.950); the launches traced: 23.7 us -> 22.1 us
  Pallas kernels: 22.4 us -> 20.8 us
    pallas_call x1, Pallas kernels: 22.4 us -> 20.8 us  [paired_call(): pl.pallas_call(paired_kernel, out_shape=jax.ShapeDtypeStruct((tokens, qw)...]
where the time goes in v3:
time: 22.6 us; the launch traced here: 22.1 us
  Pallas kernels  20.8 us (92%)
  local copies, waits for them, and re-layouts  1.32 us (6%)
    pallas_call x1, Pallas kernels, paired_call(): pl.pallas_call(paired_kernel, out_shape=jax.ShapeDtypeStruct((tokens, qw)...  20.8 us
    unnamed x1, local copies, waits for them, and re-layouts  1.32 us

profile of v3, /device:TPU:17, one launch (start us, length us, event | category | flops | bytes accessed | tf_op | source)
XLA Modules:
  0.0 22.1 jit_solution(11533136395756982053)
XLA Ops:
  0.0 20.8 %shard_map.73 = bf16[512,2048]{1,0:T(8,128)(2,1)S(1)} custom-call(s32[4,3]{1,0:T(4,128)} %list_hbm.1, bf16[512,2048]{1,0:T(8,128)(2,1)} %q_hbm.1, bf16[512,512]{1,0:T(8,128)(2,1)} %k_hbm.1, bf16[512,512]{1,0:T(8,128)(2,1)} %v_hbm.1, f32[3,2048]{1,0:T(4,128)} %qt_hbm.1, f32[3,512]{1,0:T(4,128)} %kt_hbm.1, f32[3,512]{1,0:T(4,128)} %vt_hbm.1), custom_call_target="tpu_custom_call" | custom-call | flops 1610612736 | bytes 5242880 | tf_op jit(solution)/shard_map/pallas_call | solution.py:889
  20.8 1.3 %copy.9 = bf16[512,2048]{1,0:T(8,128)(2,1)} copy(bf16[512,2048]{1,0:T(8,128)(2,1)S(1)} %shard_map.73) | data formatting | bytes 4194304

commit v4 on v3

--- a/solution.py
+++ b/solution.py
@@ -384,7 +384,8 @@
 ROWS = 4
 SUMS = ({0: (1,), 2: (3,)}, {0: (2, 1), 1: (2,)})
 SPREADS = ({1: (3, 2)}, {2: (3,)})
-SITE_STEPS = ((2, 2), (3, 3))
+FIRST_ROW_STEP = 1
+UNROLL = 4
 LATE = ((2, 3), (1, 3), (0, 2))
 
 
@@ -400,7 +401,7 @@
 def paired_kernel(
     list_hbm, q_hbm, k_hbm, v_hbm, qt_hbm, kt_hbm, vt_hbm, outb,
     list_ref, qt_ref, kt_ref, vt_ref, qpad, kvpad, kvc, qs, acc_ref, max_ref, pbuf,
-    flag_out, flag_in, chip, cand, rrow, rother, rsum, zrow, zfar, far,
+    flag_out, flag_in, chip, cand, rrow, rother, site, zfar, far_k, far_v,
     in_sem, own_sem, fl_s, fl_r, raw_s, raw_r, rim_s, rim_r, tail_s, tail_r,
     a_s, a_r, b_s, b_r, c_s, c_r, d_s, d_r, e_s, e_r, ready,
 ):
@@ -538,6 +539,8 @@
     def _():
         chip[:, 0:HALO, :] = jnp.zeros((2, HALO, hw), jnp.bfloat16)
 
+    far_k[...] = jnp.zeros(far_k.shape, jnp.bfloat16)
+
     @pl.when(jnp.logical_not(chip_next))
     def _():
         flag_in[0] = jnp.full(flag_in.shape[1:], -1, jnp.int32)
@@ -622,25 +625,33 @@
         )
 
     def to_peer_col(h):
-        return remote(rsum.at[h], zrow.at[h], c_s.at[h], c_r.at[h], peer_y)
+        return remote(site.at[h, y], site.at[h, y], c_s.at[h], c_r.at[h], peer_y)
+
+    def from_peer_col(h):
+        return remote(site.at[h, 1 - y], site.at[h, 1 - y], c_s.at[h], c_r.at[h], peer_y)
 
     def to_later(h, row, col):
         return remote(
-            rsum.at[h], zfar.at[h, o, y], d_s.at[h, row, col], d_r.at[h, o, y], at(row, col)
+            site.at[h, y], zfar.at[h, o, y], d_s.at[h, row, col], d_r.at[h, o, y], at(row, col)
         )
 
     def from_earlier(h, src, col):
         return remote(
-            rsum.at[h], zfar.at[h, src, col], d_s.at[h, 0, 0], d_r.at[h, src, col], peer_y
-        )
+            site.at[h, y], zfar.at[h, src, col], d_s.at[h, 0, 0], d_r.at[h, src, col], peer_y
+        )
+
+    def core_swap(h, core):
+        if h == 0:
+            part = far_k.at[core]
+        else:
+            part = far_v.at[pl.ds(2 * core, 2)]
+        return remote(part, part, e_s.at[h], e_r.at[h], peer_core)
 
     def to_peer_core(h):
-        mine = pl.ds(2 * c, 2)
-        return remote(far.at[h, mine], far.at[h, mine], e_s.at[h], e_r.at[h], peer_core)
+        return core_swap(h, c)
 
     def from_peer_core(h):
-        theirs = pl.ds(2 - 2 * c, 2)
-        return remote(far.at[h, theirs], far.at[h, theirs], e_s.at[h], e_r.at[h], peer_core)
+        return core_swap(h, 1 - c)
 
     def candidate_step():
         pl.when(awaited > 0)(lambda: pl.semaphore_wait(ready, awaited))
@@ -686,7 +697,7 @@
 
     def site_step(h):
         to_peer_site(h).wait_recv()
-        rsum[h] = cand[h, y] + rrow[h]
+        site[h, y] = cand[h, y] + rrow[h]
         for row in range(no):
             sources = [src for src, rows in SUMS[h].items() if row in rows]
             if sources:
@@ -696,7 +707,7 @@
                     for src in sources:
                         for col in range(2):
                             at_site(h, src, col).wait_recv()
-                            rsum[h] = rsum[h] + rother[h, src, col]
+                            site[h, y] = site[h, y] + rother[h, src, col]
 
         for src, rows in SPREADS[h].items():
 
@@ -709,9 +720,7 @@
         to_peer_col(h).start()
 
     def final_step(h):
-        to_peer_col(h).wait_recv()
-        far[h, 2 * c + y] = rsum[h]
-        far[h, 2 * c + 1 - y] = zrow[h]
+        from_peer_col(h).wait_recv()
         for src, rows in SPREADS[h].items():
             for row in rows:
 
@@ -719,16 +728,27 @@
                 def _():
                     for col in range(2):
                         from_earlier(h, src, col).wait_recv()
-                        far[h, 2 * c + col] = far[h, 2 * c + col] + zfar[h, src, col]
-
+                        zfar[h, o, col] = zfar[h, src, col] + site[h, col]
+
+        gets = functools.reduce(
+            jnp.logical_or, [o == row for rows in SPREADS[h].values() for row in rows]
+        )
+
+        def place(source):
+            for col in range(2):
+                if h == 0:
+                    far_k[c, cols_of(col), cols_of(col)] = source(col)
+                else:
+                    far_v[2 * c + col] = source(col)
+
+        pl.when(gets)(lambda: place(lambda col: zfar[h, o, col]))
+        pl.when(jnp.logical_not(gets))(lambda: place(lambda col: site[h, col]))
         to_peer_core(h).start()
 
     for n in (1, 5, 2, 6):
         loads[n].wait()
     for b in range(2, nb + 1):
         kv_conv(b)
-    candidate_step()
-
     loads[0].wait()
     loads[4].wait()
 
@@ -766,7 +786,7 @@
             q = jnp.concatenate(
                 [q[:, h * HEAD_DIM : (h + 1) * HEAD_DIM] for h in range(per_group)], 0
             )
-            qs[b, g] = q
+            qs[b, g // 2, :, cols_of(g % 2)] = q
             k = kvc[0, pl.ds(base, LOCAL * BLOCK), cols]
             v = kvc[1, pl.ds(base, LOCAL * BLOCK), cols]
             s = lax.dot_general(q, k, NT, preferred_element_type=jnp.float32)
@@ -780,61 +800,69 @@
                 p, jnp.concatenate([v, ones], 1), preferred_element_type=jnp.float32
             )
             max_ref[b, g] = jnp.broadcast_to(peak, (per_group * BLOCK, HEAD_DIM))
-            for (at_step, at_group), h in zip(SITE_STEPS, range(2)):
-                if at_group == g:
-                    pl.when(step == at_step)(functools.partial(site_step, h))
-
+
+        pl.when(step == jnp.where(o == 0, FIRST_ROW_STEP, 0))(candidate_step)
         return carry
 
     lax.fori_loop(0, nb, near, 0)
+    site_step(0)
+    site_step(1)
     final_step(0)
 
-    def distant_keys(first, b, carry):
+    def distant_keys(pair, b):
         seen = jnp.int32(0)
         for e in range(entries):
             entry = list_ref[b, e]
             seen = jnp.where((entry >= 0) & (entry <= d * nb + b - LOCAL), 1, seen)
         bias = jnp.where(seen > 0, 0.0, NEG)
+        both = lax.dot_general(qs[b, pair], far_k[pair], NT, preferred_element_type=jnp.float32)
         for n in range(2):
-            g = first + n
-            q = qs[b, g]
+            g = 2 * pair + n
+            s = both[:, cols_of(n)] + bias
             near_peak = max_ref[b, g]
-            s = lax.dot_general(q, far[0, g], NT, preferred_element_type=jnp.float32) + bias
             peak = jnp.maximum(near_peak, jnp.max(s, axis=1, keepdims=True))
             max_ref[b, g] = jnp.exp2((near_peak - peak) * SCALE)
             pbuf[b, g] = jnp.exp2((s - peak) * SCALE).astype(jnp.bfloat16)
-        return carry
-
-    def distant_values(first, b, carry):
+
+    def distant_values(pair, b):
         base = pl.multiple_of(b * BLOCK, BLOCK)
         for n in range(2):
-            g = first + n
-            both = acc_ref[b, g]
+            g = 2 * pair + n
             shrink = max_ref[b, g]
             more = jnp.dot(
                 pbuf[b, g],
-                jnp.concatenate([far[1, g], ones[:BLOCK]], 1),
+                jnp.concatenate([far_v[g], ones[:BLOCK]], 1),
                 preferred_element_type=jnp.float32,
             )
-            total = both[:, :HEAD_DIM] * shrink + more[:, :HEAD_DIM]
-            count = both[:, HEAD_DIM:] * shrink + more[:, HEAD_DIM:]
-            mixed = (total / count).astype(jnp.bfloat16)
+            total = acc_ref[b, g, :, :HEAD_DIM] * shrink + more[:, :HEAD_DIM]
+            count = acc_ref[b, g, :, HEAD_DIM:] * shrink + more[:, HEAD_DIM:]
+            inverse = pl.reciprocal(count, approx=True)
+            inverse = inverse * (2.0 - count * inverse)
+            mixed = (total * inverse).astype(jnp.bfloat16)
             for h in range(per_group):
-                col = pl.multiple_of((g * per_group + h) * HEAD_DIM, HEAD_DIM)
-                outb[pl.ds(base, BLOCK), pl.ds(col, HEAD_DIM)] = mixed[
+                head = g * per_group + h
+                outb[pl.ds(base, BLOCK), head * HEAD_DIM : (head + 1) * HEAD_DIM] = mixed[
                     h * BLOCK : (h + 1) * BLOCK
                 ]
-        return carry
-
-    mine = 2 * c
-    theirs = 2 - 2 * c
-    lax.fori_loop(0, nb, functools.partial(distant_keys, mine), 0, unroll=2)
-    from_peer_core(0).wait_recv()
-    lax.fori_loop(0, nb, functools.partial(distant_keys, theirs), 0, unroll=2)
+
+    def loop(run, pair):
+        def step(b, carry):
+            run(pair, b)
+            return carry
+
+        lax.fori_loop(0, nb, step, 0, unroll=UNROLL)
+
+    def far_stage(pair):
+        loop(distant_keys, pair)
+        loop(distant_values, pair)
+        core_swap(0, 1 - pair).wait_recv()
+        loop(distant_keys, 1 - pair)
+        core_swap(1, 1 - pair).wait_recv()
+        loop(distant_values, 1 - pair)
+
     final_step(1)
-    lax.fori_loop(0, nb, functools.partial(distant_values, mine), 0, unroll=2)
-    from_peer_core(1).wait_recv()
-    lax.fori_loop(0, nb, functools.partial(distant_values, theirs), 0, unroll=2)
+    pl.when(first_core)(functools.partial(far_stage, 0))
+    pl.when(second_core)(functools.partial(far_stage, 1))
 
     @pl.when(first_core & chip_prev)
     def _():
@@ -899,7 +927,7 @@
             pltpu.VMEM((tokens + HALO, qw), bf16),
             pltpu.VMEM((2, tokens + BLOCK + HALO, kvw), bf16),
             pltpu.VMEM((2, tokens + BLOCK, kvw), bf16),
-            pltpu.VMEM((nb, groups, rows, HEAD_DIM), bf16),
+            pltpu.VMEM((nb, groups // 2, rows, 2 * HEAD_DIM), bf16),
             pltpu.VMEM((nb, groups, rows, 2 * HEAD_DIM), f32),
             pltpu.VMEM((nb, groups, rows, HEAD_DIM), f32),
             pltpu.VMEM((nb, groups, rows, BLOCK), bf16),
@@ -909,10 +937,10 @@
             pltpu.VMEM((2, 2, *piece), bf16),
             pltpu.VMEM((2, *piece), bf16),
             pltpu.VMEM((2, ROWS, 2, *piece), bf16),
-            pltpu.VMEM((2, *piece), bf16),
-            pltpu.VMEM((2, *piece), bf16),
+            pltpu.VMEM((2, 2, *piece), bf16),
             pltpu.VMEM((2, ROWS, 2, *piece), bf16),
-            pltpu.VMEM((2, groups, BLOCK, HEAD_DIM), bf16),
+            pltpu.VMEM((groups // 2, 2 * BLOCK, hw), bf16),
+            pltpu.VMEM((groups, BLOCK, HEAD_DIM), bf16),
             dma((7,)),
             dma((2,)),
             dma((3,)),

time: 22.6 us -> 21.5 us (0.951); the launches traced: 22.1 us -> 21.4 us
  Pallas kernels: 20.8 us -> 20 us
    pallas_call x1, Pallas kernels: 20.8 us -> 20 us  [paired_call(): pl.pallas_call(paired_kernel, out_shape=jax.ShapeDtypeStruct((tokens, qw)...]
where the time goes in v4:
time: 21.5 us; the launch traced here: 21.4 us
  Pallas kernels  20 us (93%)
  local copies, waits for them, and re-layouts  1.32 us (6%)
    pallas_call x1, Pallas kernels, paired_call(): pl.pallas_call(paired_kernel, out_shape=jax.ShapeDtypeStruct((tokens, qw)...  20 us
    unnamed x1, local copies, waits for them, and re-layouts  1.32 us

profile of v4, /device:TPU:17, one launch (start us, length us, event | category | flops | bytes accessed | tf_op | source)
XLA Modules:
  0.0 21.4 jit_solution(16136296347747799133)
XLA Ops:
  0.0 20.0 %shard_map.73 = bf16[512,2048]{1,0:T(8,128)(2,1)S(1)} custom-call(s32[4,3]{1,0:T(4,128)} %list_hbm.1, bf16[512,2048]{1,0:T(8,128)(2,1)} %q_hbm.1, bf16[512,512]{1,0:T(8,128)(2,1)} %k_hbm.1, bf16[512,512]{1,0:T(8,128)(2,1)} %v_hbm.1, f32[3,2048]{1,0:T(4,128)} %qt_hbm.1, f32[3,512]{1,0:T(4,128)} %kt_hbm.1, f32[3,512]{1,0:T(4,128)} %vt_hbm.1), custom_call_target="tpu_custom_call" | custom-call | flops 1610612736 | bytes 5242880 | tf_op jit(solution)/shard_map/pallas_call | solution.py:917
  20.0 1.3 %copy.9 = bf16[512,2048]{1,0:T(8,128)(2,1)} copy(bf16[512,2048]{1,0:T(8,128)(2,1)S(1)} %shard_map.73) | data formatting | bytes 4194304

commit v5 on v4

--- a/solution.py
+++ b/solution.py
@@ -382,9 +382,12 @@
 
 
 ROWS = 4
-SUMS = ({0: (1,), 2: (3,)}, {0: (2, 1), 1: (2,)})
-SPREADS = ({1: (3, 2)}, {2: (3,)})
+SUMS = ({0: (1,), 2: (3,)}, {0: (2,), 1: (2,)})
+SPREADS = ({1: (3, 2)}, {2: (3, 1)})
+TAKEN = ((), (1,))
 FIRST_ROW_STEP = 1
+SITE_AFTER = (2, 2)
+LATE_TAILS = False
 UNROLL = 4
 LATE = ((2, 3), (1, 3), (0, 2))
 
@@ -469,10 +472,10 @@
     greet(peer_y)
 
     late_next = (y == 1) & functools.reduce(
-        jnp.logical_or, [o == row for row in range(no - 1) if (row, row + 1) in LATE]
+        jnp.logical_or, [o == row for row in range(no - 1) if (row, row + 1) in LATE], o < 0
     )
     late_prev = (y == 0) & functools.reduce(
-        jnp.logical_or, [o == row + 1 for row in range(no - 1) if (row, row + 1) in LATE]
+        jnp.logical_or, [o == row + 1 for row in range(no - 1) if (row, row + 1) in LATE], o < 0
     )
 
     @pl.when(chip_next)
@@ -523,12 +526,18 @@
         ]
         for k in range(2)
     ]
-    tail_rows = pl.ds(tokens - before, before)
+    body_rows = pl.ds(tokens - before, BLOCK)
+
+    def to_next(n, src, dst):
+        return remote(src, dst, tail_s.at[n], tail_r.at[n], next_device)
+
+    edges = [
+        to_next(h, x.at[rim], kvpad.at[h, pl.ds(BLOCK, HALO)]) for h, x in enumerate((k_hbm, v_hbm))
+    ]
     tails = [
-        remote(k_hbm.at[tail_rows], kvpad.at[0, pl.ds(0, before)], tail_s.at[0], tail_r.at[0], next_device),
-        remote(v_hbm.at[tail_rows], kvpad.at[1, pl.ds(0, before)], tail_s.at[1], tail_r.at[1], next_device),
-        remote(q_hbm.at[rim], qpad.at[pl.ds(0, HALO)], tail_s.at[2], tail_r.at[2], next_device),
-    ]
+        to_next(2 + h, x.at[body_rows], kvpad.at[h, pl.ds(0, BLOCK)])
+        for h, x in enumerate((k_hbm, v_hbm))
+    ] + [to_next(4, q_hbm.at[rim], qpad.at[pl.ds(0, HALO)])]
 
     @pl.when(jnp.logical_not(has_prev))
     def _():
@@ -596,11 +605,19 @@
 
         @pl.when(has_next)
         def _():
+            for copy in edges:
+                copy.start()
+
+    def tail_sends():
+        @pl.when(has_next)
+        def _():
             for copy in tails:
                 copy.start()
 
     held_back = sends_on & late_next
     pl.when(jnp.logical_not(held_back))(next_sends)
+    if not LATE_TAILS:
+        pl.when(jnp.logical_not(held_back))(tail_sends)
 
     def kv_conv(b):
         rows = slice(b * BLOCK, b * BLOCK + before)
@@ -652,6 +669,9 @@
 
     def from_peer_core(h):
         return core_swap(h, 1 - c)
+
+    def sums_own(h):
+        return functools.reduce(jnp.logical_and, [o != row for row in TAKEN[h]], o >= 0)
 
     def candidate_step():
         pl.when(awaited > 0)(lambda: pl.semaphore_wait(ready, awaited))
@@ -693,9 +713,17 @@
                         for col in range(2):
                             to_site(h, row, col).start()
 
-            to_peer_site(h).start()
+            pl.when(sums_own(h))(to_peer_site(h).start)
+
+        if LATE_TAILS:
+            tail_sends()
+        else:
+            pl.when(held_back)(tail_sends)
 
     def site_step(h):
+        pl.when(sums_own(h))(functools.partial(own_site_step, h))
+
+    def own_site_step(h):
         to_peer_site(h).wait_recv()
         site[h, y] = cand[h, y] + rrow[h]
         for row in range(no):
@@ -720,7 +748,7 @@
         to_peer_col(h).start()
 
     def final_step(h):
-        from_peer_col(h).wait_recv()
+        pl.when(sums_own(h))(from_peer_col(h).wait_recv)
         for src, rows in SPREADS[h].items():
             for row in rows:
 
@@ -728,7 +756,10 @@
                 def _():
                     for col in range(2):
                         from_earlier(h, src, col).wait_recv()
-                        zfar[h, o, col] = zfar[h, src, col] + site[h, col]
+                        if row in TAKEN[h]:
+                            zfar[h, o, col] = zfar[h, src, col]
+                        else:
+                            zfar[h, o, col] = zfar[h, src, col] + site[h, col]
 
         gets = functools.reduce(
             jnp.logical_or, [o == row for rows in SPREADS[h].values() for row in rows]
@@ -764,8 +795,8 @@
         def _():
             @pl.when(has_prev)
             def _():
-                tails[0].wait_recv()
-                tails[1].wait_recv()
+                for copy in edges:
+                    copy.wait_recv()
 
             kv_conv(1)
 
@@ -773,7 +804,8 @@
         def _():
             @pl.when(has_prev)
             def _():
-                tails[2].wait_recv()
+                for copy in tails:
+                    copy.wait_recv()
 
             kv_conv(0)
 
@@ -802,11 +834,15 @@
             max_ref[b, g] = jnp.broadcast_to(peak, (per_group * BLOCK, HEAD_DIM))
 
         pl.when(step == jnp.where(o == 0, FIRST_ROW_STEP, 0))(candidate_step)
+        for h in range(2):
+            if SITE_AFTER[h] is not None:
+                pl.when(step == SITE_AFTER[h])(functools.partial(site_step, h))
         return carry
 
     lax.fori_loop(0, nb, near, 0)
-    site_step(0)
-    site_step(1)
+    for h in range(2):
+        if SITE_AFTER[h] is None:
+            site_step(h)
     final_step(0)
 
     def distant_keys(pair, b):
@@ -881,13 +917,17 @@
 
     @pl.when(has_next)
     def _():
-        for copy in tails:
+        for copy in edges + tails:
             copy.wait_send()
 
     for h in range(2):
         raws[h].wait_send()
-        to_peer_site(h).wait_send()
-        to_peer_col(h).wait_send()
+
+        @pl.when(sums_own(h))
+        def _():
+            to_peer_site(h).wait_send()
+            to_peer_col(h).wait_send()
+
         to_peer_core(h).wait_send()
 
         for table, copy in ((SUMS, to_site), (SPREADS, to_later)):
@@ -949,8 +989,8 @@
             dma((2,)),
             dma((2, 2)),
             dma((2,)),
-            dma((3,)),
-            dma((3,)),
+            dma((5,)),
+            dma((5,)),
             dma((2,)),
             dma((2,)),
             dma((2, ROWS, 2)),

time: 21.5 us -> 21.1 us (0.981)
  the two profiles are of different devices: /device:TPU:17 before, /device:TPU:9 now
where the time goes in v5:
time: 21.1 us; the launch traced here: 21 us
  Pallas kernels  19.7 us (93%)
  local copies, waits for them, and re-layouts  1.32 us (6%)
    pallas_call x1, Pallas kernels, paired_call(): pl.pallas_call(paired_kernel, out_shape=jax.ShapeDtypeStruct((tokens, qw)...  19.7 us
    unnamed x1, local copies, waits for them, and re-layouts  1.32 us

profile of v5, /device:TPU:9, one launch (start us, length us, event | category | flops | bytes accessed | tf_op | source)
XLA Modules:
  0.0 21.0 jit_solution(4487830393864910457)
XLA Ops:
  0.0 19.7 %shard_map.73 = bf16[512,2048]{1,0:T(8,128)(2,1)S(1)} custom-call(s32[4,3]{1,0:T(4,128)} %list_hbm.1, bf16[512,2048]{1,0:T(8,128)(2,1)} %q_hbm.1, bf16[512,512]{1,0:T(8,128)(2,1)} %k_hbm.1, bf16[512,512]{1,0:T(8,128)(2,1)} %v_hbm.1, f32[3,2048]{1,0:T(4,128)} %qt_hbm.1, f32[3,512]{1,0:T(4,128)} %kt_hbm.1, f32[3,512]{1,0:T(4,128)} %vt_hbm.1), custom_call_target="tpu_custom_call" | custom-call | flops 1610612736 | bytes 5242880 | tf_op jit(solution)/shard_map/pallas_call | solution.py:957
  19.7 1.3 %copy.9 = bf16[512,2048]{1,0:T(8,128)(2,1)} copy(bf16[512,2048]{1,0:T(8,128)(2,1)S(1)} %shard_map.73) | data formatting | bytes 4194304

commit v6 on v5

--- a/solution.py
+++ b/solution.py
@@ -388,7 +388,6 @@
 FIRST_ROW_STEP = 1
 SITE_AFTER = (2, 2)
 LATE_TAILS = False
-UNROLL = 4
 LATE = ((2, 3), (1, 3), (0, 2))
 
 
@@ -401,10 +400,77 @@
     return [r for r in range(ROWS) if row in dests(r, late)]
 
 
+def distant_keys(qs, peaks, max_ref, pbuf, far_k, bias_ref, pair, b):
+    both = lax.dot_general(qs[b, pair], far_k[pair], NT, preferred_element_type=jnp.float32)
+    bias = bias_ref[b : b + 1, :]
+    for n in range(2):
+        g = 2 * pair + n
+        s = both[:, n * BLOCK : (n + 1) * BLOCK] + bias
+        near_peak = peaks[b, g]
+        peak = jnp.maximum(near_peak, jnp.max(s, axis=1, keepdims=True))
+        max_ref[b, g] = jnp.exp2((near_peak - peak) * SCALE)
+        pbuf[b, g] = jnp.exp2((s - peak) * SCALE).astype(jnp.bfloat16)
+
+
+def distant_values(acc_ref, max_ref, pbuf, far_v, pair, b, dst, first_head):
+    per_group = acc_ref.shape[2] // BLOCK
+    ones = jnp.ones((BLOCK, HEAD_DIM), jnp.bfloat16)
+    for n in range(2):
+        g = 2 * pair + n
+        shrink = max_ref[b, g]
+        more = jnp.dot(
+            pbuf[b, g],
+            jnp.concatenate([far_v[g], ones], 1),
+            preferred_element_type=jnp.float32,
+        )
+        total = acc_ref[b, g, :, :HEAD_DIM] * shrink + more[:, :HEAD_DIM]
+        count = acc_ref[b, g, :, HEAD_DIM:] * shrink + more[:, HEAD_DIM:]
+        inverse = pl.reciprocal(count, approx=True)
+        inverse = inverse * (2.0 - count * inverse)
+        mixed = (total * inverse).astype(jnp.bfloat16)
+        for h in range(per_group):
+            head = first_head + n * per_group + h
+            dst[b * BLOCK : (b + 1) * BLOCK, head * HEAD_DIM : (head + 1) * HEAD_DIM] = mixed[
+                h * BLOCK : (h + 1) * BLOCK
+            ]
+
+
+def other_half_kernel(
+    own_out, qs, acc_ref, peaks, far_k, far_v, bias_ref, out, max_ref, pbuf, half_out, own_sem, out_sem
+):
+    nb = qs.shape[0]
+    tokens, qw = own_out.shape
+    wide = qw // 2
+    c = lax.rem(lax.axis_index("inner"), 2)
+
+    def half(pair):
+        own_cols = pl.ds((1 - pair) * wide, wide)
+        cols = pl.ds(pair * wide, wide)
+        own_copy = pltpu.make_async_copy(own_out.at[:, own_cols], out.at[:, own_cols], own_sem)
+        own_copy.start()
+        for b in range(nb):
+            distant_keys(qs, peaks, max_ref, pbuf, far_k, bias_ref, pair, b)
+        copies = []
+        for b in range(nb):
+            rows = pl.ds(b * BLOCK, BLOCK)
+            distant_values(acc_ref, max_ref, pbuf, far_v, pair, b, half_out, 0)
+            copies.append(
+                pltpu.make_async_copy(half_out.at[rows], out.at[rows, cols], out_sem.at[b])
+            )
+            copies[-1].start()
+        for copy in copies:
+            copy.wait()
+        own_copy.wait()
+
+    pl.when(c == 0)(lambda: half(1))
+    pl.when(c == 1)(lambda: half(0))
+
+
 def paired_kernel(
-    list_hbm, q_hbm, k_hbm, v_hbm, qt_hbm, kt_hbm, vt_hbm, outb,
-    list_ref, qt_ref, kt_ref, vt_ref, qpad, kvpad, kvc, qs, acc_ref, max_ref, pbuf,
-    flag_out, flag_in, chip, cand, rrow, rother, site, zfar, far_k, far_v,
+    list_hbm, q_hbm, k_hbm, v_hbm, qt_hbm, kt_hbm, vt_hbm,
+    outb, qs, acc_ref, max_ref, far_k, far_v, bias_ref,
+    list_ref, qt_ref, kt_ref, vt_ref, qpad, kvpad, kvc, pbuf,
+    flag_out, flag_in, chip, cand, rrow, rother, site, zfar,
     in_sem, own_sem, fl_s, fl_r, raw_s, raw_r, rim_s, rim_r, tail_s, tail_r,
     a_s, a_r, b_s, b_r, c_s, c_r, d_s, d_r, e_s, e_r, ready,
 ):
@@ -845,60 +911,26 @@
             site_step(h)
     final_step(0)
 
-    def distant_keys(pair, b):
+    for b in range(nb):
         seen = jnp.int32(0)
         for e in range(entries):
             entry = list_ref[b, e]
             seen = jnp.where((entry >= 0) & (entry <= d * nb + b - LOCAL), 1, seen)
-        bias = jnp.where(seen > 0, 0.0, NEG)
-        both = lax.dot_general(qs[b, pair], far_k[pair], NT, preferred_element_type=jnp.float32)
-        for n in range(2):
-            g = 2 * pair + n
-            s = both[:, cols_of(n)] + bias
-            near_peak = max_ref[b, g]
-            peak = jnp.maximum(near_peak, jnp.max(s, axis=1, keepdims=True))
-            max_ref[b, g] = jnp.exp2((near_peak - peak) * SCALE)
-            pbuf[b, g] = jnp.exp2((s - peak) * SCALE).astype(jnp.bfloat16)
-
-    def distant_values(pair, b):
-        base = pl.multiple_of(b * BLOCK, BLOCK)
-        for n in range(2):
-            g = 2 * pair + n
-            shrink = max_ref[b, g]
-            more = jnp.dot(
-                pbuf[b, g],
-                jnp.concatenate([far_v[g], ones[:BLOCK]], 1),
-                preferred_element_type=jnp.float32,
-            )
-            total = acc_ref[b, g, :, :HEAD_DIM] * shrink + more[:, :HEAD_DIM]
-            count = acc_ref[b, g, :, HEAD_DIM:] * shrink + more[:, HEAD_DIM:]
-            inverse = pl.reciprocal(count, approx=True)
-            inverse = inverse * (2.0 - count * inverse)
-            mixed = (total * inverse).astype(jnp.bfloat16)
-            for h in range(per_group):
-                head = g * per_group + h
-                outb[pl.ds(base, BLOCK), head * HEAD_DIM : (head + 1) * HEAD_DIM] = mixed[
-                    h * BLOCK : (h + 1) * BLOCK
-                ]
-
-    def loop(run, pair):
-        def step(b, carry):
-            run(pair, b)
-            return carry
-
-        lax.fori_loop(0, nb, step, 0, unroll=UNROLL)
+        bias_ref[b : b + 1, :] = jnp.full((1, 128), jnp.where(seen > 0, 0.0, NEG), jnp.float32)
+    if nb < bias_ref.shape[0]:
+        bias_ref[nb:, :] = jnp.zeros((bias_ref.shape[0] - nb, 128), jnp.float32)
 
     def far_stage(pair):
-        loop(distant_keys, pair)
-        loop(distant_values, pair)
-        core_swap(0, 1 - pair).wait_recv()
-        loop(distant_keys, 1 - pair)
-        core_swap(1, 1 - pair).wait_recv()
-        loop(distant_values, 1 - pair)
+        for b in range(nb):
+            distant_keys(qs, max_ref, max_ref, pbuf, far_k, bias_ref, pair, b)
+        for b in range(nb):
+            distant_values(acc_ref, max_ref, pbuf, far_v, pair, b, outb, 2 * pair * per_group)
 
     final_step(1)
     pl.when(first_core)(functools.partial(far_stage, 0))
     pl.when(second_core)(functools.partial(far_stage, 1))
+    for h in range(2):
+        from_peer_core(h).wait_recv()
 
     @pl.when(first_core & chip_prev)
     def _():
@@ -954,11 +986,21 @@
     bf16, f32 = jnp.bfloat16, jnp.float32
     hbm_spec = pl.BlockSpec(memory_space=pltpu.HBM)
     scores = nb * groups * rows * (LOCAL + 1) * BLOCK
-    return pl.pallas_call(
+    vmem_spec = pl.BlockSpec(memory_space=pltpu.VMEM)
+    partial_shapes = [
+        ((tokens, qw), bf16),
+        ((nb, groups // 2, rows, 2 * HEAD_DIM), bf16),
+        ((nb, groups, rows, 2 * HEAD_DIM), f32),
+        ((nb, groups, rows, HEAD_DIM), f32),
+        ((groups // 2, 2 * BLOCK, hw), bf16),
+        ((groups, BLOCK, HEAD_DIM), bf16),
+        ((max(8, nb), 128), f32),
+    ]
+    partial = pl.pallas_call(
         paired_kernel,
-        out_shape=jax.ShapeDtypeStruct((tokens, qw), bf16),
+        out_shape=[jax.ShapeDtypeStruct(*x) for x in partial_shapes],
         in_specs=[hbm_spec] * 7,
-        out_specs=pl.BlockSpec(memory_space=pltpu.VMEM),
+        out_specs=[vmem_spec] * 7,
         scratch_shapes=[
             pltpu.SMEM(block_list.shape, jnp.int32),
             pltpu.VMEM(q_taps.shape, f32),
@@ -967,9 +1009,6 @@
             pltpu.VMEM((tokens + HALO, qw), bf16),
             pltpu.VMEM((2, tokens + BLOCK + HALO, kvw), bf16),
             pltpu.VMEM((2, tokens + BLOCK, kvw), bf16),
-            pltpu.VMEM((nb, groups // 2, rows, 2 * HEAD_DIM), bf16),
-            pltpu.VMEM((nb, groups, rows, 2 * HEAD_DIM), f32),
-            pltpu.VMEM((nb, groups, rows, HEAD_DIM), f32),
             pltpu.VMEM((nb, groups, rows, BLOCK), bf16),
             pltpu.VMEM((8, hw), jnp.int32),
             pltpu.VMEM((2, 8, hw), jnp.int32),
@@ -979,8 +1018,6 @@
             pltpu.VMEM((2, ROWS, 2, *piece), bf16),
             pltpu.VMEM((2, 2, *piece), bf16),
             pltpu.VMEM((2, ROWS, 2, *piece), bf16),
-            pltpu.VMEM((groups // 2, 2 * BLOCK, hw), bf16),
-            pltpu.VMEM((groups, BLOCK, HEAD_DIM), bf16),
             dma((7,)),
             dma((2,)),
             dma((3,)),
@@ -1004,7 +1041,7 @@
             pltpu.SemaphoreType.REGULAR,
         ],
         compiler_params=pltpu.CompilerParams(
-            collective_id=0, has_side_effects=True, vmem_limit_bytes=48 * 1024 * 1024
+            collective_id=0, has_side_effects=True, vmem_limit_bytes=36 * 1024 * 1024
         ),
         cost_estimate=pl.CostEstimate(
             flops=4 * scores * HEAD_DIM,
@@ -1012,6 +1049,23 @@
             transcendentals=scores,
         ),
     )(*arrays)
+    return pl.pallas_call(
+        other_half_kernel,
+        out_shape=jax.ShapeDtypeStruct((tokens, qw), bf16),
+        in_specs=[vmem_spec] * 7,
+        out_specs=hbm_spec,
+        scratch_shapes=[
+            pltpu.VMEM((nb, groups, rows, HEAD_DIM), f32),
+            pltpu.VMEM((nb, groups, rows, BLOCK), bf16),
+            pltpu.VMEM((tokens, qw // 2), bf16),
+            dma,
+            dma((nb,)),
+        ],
+        compiler_params=pltpu.CompilerParams(vmem_limit_bytes=36 * 1024 * 1024),
+        cost_estimate=pl.CostEstimate(
+            flops=scores * HEAD_DIM, bytes_accessed=2 * tokens * qw, transcendentals=scores // 6
+        ),
+    )(*partial)
 
 
 def body(q_proj, k_proj, v_proj, q_taps, k_taps, v_taps, block_list):

time: 21.1 us -> 20.5 us (0.972)
  local copies, waits for them, and re-layouts: 1.32 us -> 0 us
  Pallas kernels: 19.7 us -> 20.4 us
    unnamed x1 -> x0, local copies, waits for them, and re-layouts: 1.32 us -> none
    pallas_call x1 -> x2, Pallas kernels: 19.7 us -> 20.4 us  [the longest x1 18 us: paired_call(): pl.pallas_call(paired_kernel, out_shape=[jax.ShapeDtypeStruct(*x) for x i...]
where the time goes in v6:
time: 20.5 us; the launch traced here: 20.4 us
  Pallas kernels  20.4 us (100%)
    pallas_call x1, Pallas kernels, paired_call(): pl.pallas_call(paired_kernel, out_shape=[jax.ShapeDtypeStruct(*x) for x i...  18 us
    pallas_call x1, Pallas kernels, paired_call(): pl.pallas_call(other_half_kernel, out_shape=jax.ShapeDtypeStruct((tokens,...  2.39 us

profile of v6, /device:TPU:9, one launch (start us, length us, event | category | flops | bytes accessed | tf_op | source)
XLA Modules:
  0.0 20.4 jit_solution(1560612025804616453)
XLA Ops:
  0.0 18.0 %shard_map.73 = (bf16[512,2048]{1,0:T(8,128)(2,1)S(1)}, bf16[4,2,512,256]{3,2,1,0:T(8,128)(2,1)S(1)}, f32[4,4,512,256]{3,2,1,0:T(8,128)S(1)}, f32[4,4,512,128]{3...) custom-call(s32[4,3]{1,0:T(4,128)} %list_hbm.1, ...), custom_call_target="tpu_custom_call" | custom-call | flops 1610612736 | bytes 5242880 | tf_op jit(solution)/shard_map/pallas_call | solution.py:999
  18.0 2.4 %shard_map.74 = bf16[512,2048]{1,0:T(8,128)(2,1)} custom-call(bf16[512,2048]{1,0:T(8,128)(2,1)S(1)} %get-tuple-element.12.own_out, bf16[4,2,512,256]{3,2,1,0:T(8,128)(2,1)S(1)} %get-tuple-element.13.qs, f32[4,4,512,256]{3,2,1,0:T(8,128)S(1)} %get-tuple-element.14.acc_ref, f32[4,4,512,128]{3,2,1,0:T(8,128)S(1)} %get-tuple-element.15.peaks, ...), custom_call_target="tpu_custom_call" | custom-call | flops 402653184 | bytes 2097152 | tf_op jit(solution)/shard_map/pallas_call | solution.py:1052

commit v7 on v6

--- a/solution.py
+++ b/solution.py
@@ -923,10 +923,10 @@
     def far_stage(pair):
         for b in range(nb):
             distant_keys(qs, max_ref, max_ref, pbuf, far_k, bias_ref, pair, b)
+        final_step(1)
         for b in range(nb):
             distant_values(acc_ref, max_ref, pbuf, far_v, pair, b, outb, 2 * pair * per_group)
 
-    final_step(1)
     pl.when(first_core)(functools.partial(far_stage, 0))
     pl.when(second_core)(functools.partial(far_stage, 1))
     for h in range(2):

time: 20.5 us -> 20.2 us (0.985)
  the two profiles are of different devices: /device:TPU:9 before, /device:TPU:17 now
where the time goes in v7:
time: 20.2 us; the launch traced here: 20.1 us
  Pallas kernels  20.1 us (100%)
    pallas_call x1, Pallas kernels, paired_call(): pl.pallas_call(paired_kernel, out_shape=[jax.ShapeDtypeStruct(*x) for x i...  17.7 us
    pallas_call x1, Pallas kernels, paired_call(): pl.pallas_call(other_half_kernel, out_shape=jax.ShapeDtypeStruct((tokens,...  2.39 us

profile of v7, /device:TPU:17, one launch (start us, length us, event | category | flops | bytes accessed | tf_op | source)
XLA Modules:
  0.0 20.1 jit_solution(15952457869675069264)
XLA Ops:
  0.0 17.7 %shard_map.73 = (bf16[512,2048]{1,0:T(8,128)(2,1)S(1)}, bf16[4,2,512,256]{3,2,1,0:T(8,128)(2,1)S(1)}, f32[4,4,512,256]{3,2,1,0:T(8,128)S(1)}, f32[4,4,512,128]{3...) custom-call(s32[4,3]{1,0:T(4,128)} %list_hbm.1, ...), custom_call_target="tpu_custom_call" | custom-call | flops 1610612736 | bytes 5242880 | tf_op jit(solution)/shard_map/pallas_call | solution.py:999
  17.7 2.4 %shard_map.74 = bf16[512,2048]{1,0:T(8,128)(2,1)} custom-call(bf16[512,2048]{1,0:T(8,128)(2,1)S(1)} %get-tuple-element.12.own_out, bf16[4,2,512,256]{3,2,1,0:T(8,128)(2,1)S(1)} %get-tuple-element.13.qs, f32[4,4,512,256]{3,2,1,0:T(8,128)S(1)} %get-tuple-element.14.acc_ref, f32[4,4,512,128]{3,2,1,0:T(8,128)S(1)} %get-tuple-element.15.peaks, ...), custom_call_target="tpu_custom_call" | custom-call | flops 402653184 | bytes 2097152 | tf_op jit(solution)/shard_map/pallas_call | solution.py:1052

commit v8 on v7

--- a/solution.py
+++ b/solution.py
@@ -425,9 +425,7 @@
         )
         total = acc_ref[b, g, :, :HEAD_DIM] * shrink + more[:, :HEAD_DIM]
         count = acc_ref[b, g, :, HEAD_DIM:] * shrink + more[:, HEAD_DIM:]
-        inverse = pl.reciprocal(count, approx=True)
-        inverse = inverse * (2.0 - count * inverse)
-        mixed = (total * inverse).astype(jnp.bfloat16)
+        mixed = (total / count).astype(jnp.bfloat16)
         for h in range(per_group):
             head = first_head + n * per_group + h
             dst[b * BLOCK : (b + 1) * BLOCK, head * HEAD_DIM : (head + 1) * HEAD_DIM] = mixed[

time: 20.2 us -> 20.1 us (level)
  no operation moved by 1% of the time
where the time goes in v8:
time: 20.1 us; the launch traced here: 19.9 us
  Pallas kernels  19.9 us (99%)
    pallas_call x1, Pallas kernels, paired_call(): pl.pallas_call(paired_kernel, out_shape=[jax.ShapeDtypeStruct(*x) for x i...  17.7 us
    pallas_call x1, Pallas kernels, paired_call(): pl.pallas_call(other_half_kernel, out_shape=jax.ShapeDtypeStruct((tokens,...  2.24 us

profile of v8, /device:TPU:17, one launch (start us, length us, event | category | flops | bytes accessed | tf_op | source)
XLA Modules:
  0.0 19.9 jit_solution(5179058511350399050)
XLA Ops:
  0.0 17.7 %shard_map.73 = (bf16[512,2048]{1,0:T(8,128)(2,1)S(1)}, bf16[4,2,512,256]{3,2,1,0:T(8,128)(2,1)S(1)}, f32[4,4,512,256]{3,2,1,0:T(8,128)S(1)}, f32[4,4,512,128]{3...) custom-call(s32[4,3]{1,0:T(4,128)} %list_hbm.1, ...), custom_call_target="tpu_custom_call" | custom-call | flops 1610612736 | bytes 5242880 | tf_op jit(solution)/shard_map/pallas_call | solution.py:997
  17.7 2.2 %shard_map.74 = bf16[512,2048]{1,0:T(8,128)(2,1)} custom-call(bf16[512,2048]{1,0:T(8,128)(2,1)S(1)} %get-tuple-element.12.own_out, bf16[4,2,512,256]{3,2,1,0:T(8,128)(2,1)S(1)} %get-tuple-element.13.qs, f32[4,4,512,256]{3,2,1,0:T(8,128)S(1)} %get-tuple-element.14.acc_ref, f32[4,4,512,128]{3,2,1,0:T(8,128)S(1)} %get-tuple-element.15.peaks, ...), custom_call_target="tpu_custom_call" | custom-call | flops 402653184 | bytes 2097152 | tf_op jit(solution)/shard_map/pallas_call | solution.py:1050

commit v9 on v8

--- a/solution.py
+++ b/solution.py
@@ -446,10 +446,11 @@
         cols = pl.ds(pair * wide, wide)
         own_copy = pltpu.make_async_copy(own_out.at[:, own_cols], out.at[:, own_cols], own_sem)
         own_copy.start()
+        copies = []
+        distant_keys(qs, peaks, max_ref, pbuf, far_k, bias_ref, pair, 0)
         for b in range(nb):
-            distant_keys(qs, peaks, max_ref, pbuf, far_k, bias_ref, pair, b)
-        copies = []
-        for b in range(nb):
+            if b + 1 < nb:
+                distant_keys(qs, peaks, max_ref, pbuf, far_k, bias_ref, pair, b + 1)
             rows = pl.ds(b * BLOCK, BLOCK)
             distant_values(acc_ref, max_ref, pbuf, far_v, pair, b, half_out, 0)
             copies.append(

time: 20.1 us -> 20.1 us (level)
  no operation moved by 1% of the time
where the time goes in v9:
time: 20.1 us; the launch traced here: 19.9 us
  Pallas kernels  19.9 us (99%)
    pallas_call x1, Pallas kernels, paired_call(): pl.pallas_call(paired_kernel, out_shape=[jax.ShapeDtypeStruct(*x) for x i...  17.7 us
    pallas_call x1, Pallas kernels, paired_call(): pl.pallas_call(other_half_kernel, out_shape=jax.ShapeDtypeStruct((tokens,...  2.24 us

profile of v9, /device:TPU:17, one launch (start us, length us, event | category | flops | bytes accessed | tf_op | source)
XLA Modules:
  0.0 19.9 jit_solution(16287842095179939698)
XLA Ops:
  0.0 17.7 %shard_map.73 = (bf16[512,2048]{1,0:T(8,128)(2,1)S(1)}, bf16[4,2,512,256]{3,2,1,0:T(8,128)(2,1)S(1)}, f32[4,4,512,256]{3,2,1,0:T(8,128)S(1)}, f32[4,4,512,128]{3...) custom-call(s32[4,3]{1,0:T(4,128)} %list_hbm.1, ...), custom_call_target="tpu_custom_call" | custom-call | flops 1610612736 | bytes 5242880 | tf_op jit(solution)/shard_map/pallas_call | solution.py:998
  17.7 2.2 %shard_map.74 = bf16[512,2048]{1,0:T(8,128)(2,1)} custom-call(bf16[512,2048]{1,0:T(8,128)(2,1)S(1)} %get-tuple-element.12.own_out, bf16[4,2,512,256]{3,2,1,0:T(8,128)(2,1)S(1)} %get-tuple-element.13.qs, f32[4,4,512,256]{3,2,1,0:T(8,128)S(1)} %get-tuple-element.14.acc_ref, f32[4,4,512,128]{3,2,1,0:T(8,128)S(1)} %get-tuple-element.15.peaks, ...), custom_call_target="tpu_custom_call" | custom-call | flops 402653184 | bytes 2097152 | tf_op jit(solution)/shard_map/pallas_call | solution.py:1051
